TPU v7x, 32 devices: a whole 2x2x4 slice. The times are simulated.
32 devices in a mesh: dp: 4 (over x, core), fsdp: 8 (over z, y).
Axes of the slice: x: 2, y: 2, z: 4, core: 2. Of those that a mesh axis runs over, the one named last changes fastest.
Arguments:
- tokens: bfloat16 [16384, 1024], P(('dp', 'fsdp')), may hold values from -6 to 6
- segments: int32 [32, 512], P(('dp', 'fsdp')), may hold values from 0 to 3, never falling along the last dimension, each value on 1 to 256 neighbouring positions
- mixer_gain: bfloat16 [1024], P('fsdp'), may hold values from 0.099609375 to 1.8984375
- in_weight: bfloat16 [1024, 3072], P('fsdp', 'dp'), may hold values from -0.1875 to 0.1875
- conv_kernel: bfloat16 [1024, 3], P('fsdp'), may hold values from -3.5 to 3.5
- out_weight: bfloat16 [1024, 1024], P('fsdp', 'dp'), may hold values from -0.1875 to 0.1875
- ffn_gain: bfloat16 [1024], P('fsdp'), may hold values from 0.099609375 to 1.8984375
- gate_weight: bfloat16 [1024, 4608], P('fsdp', 'dp'), may hold values from -0.1875 to 0.1875
- up_weight: bfloat16 [1024, 4608], P('fsdp', 'dp'), may hold values from -0.1875 to 0.1875
- down_weight: bfloat16 [1024, 4608], P('fsdp', 'dp'), may hold values from -0.09375 to 0.09375
- cotangent: bfloat16 [16384, 1024], P(('dp', 'fsdp')), may hold values from -6 to 6
Outputs:
- output: bfloat16 [16384, 1024], P(('dp', 'fsdp'))
- input_grad: float32 [16384, 1024], P(('dp', 'fsdp'))
- mixer_gain_grad: float32 [1024], P('fsdp')
- in_weight_grad: float32 [1024, 3072], P('fsdp', 'dp')
- conv_kernel_grad: float32 [1024, 3], P('fsdp')
- out_weight_grad: float32 [1024, 1024], P('fsdp', 'dp')
- ffn_gain_grad: float32 [1024], P('fsdp')
- gate_weight_grad: float32 [1024, 4608], P('fsdp', 'dp')
- up_weight_grad: float32 [1024, 4608], P('fsdp', 'dp')
- down_weight_grad: float32 [1024, 4608], P('fsdp', 'dp')
Inputs may be any that keep to these rules, and one draw needn't show every extreme that they name: `segments`: in each sequence the document numbers never fall, start at 0, and each document has 1 to 256 tokens, one exactly 256.
All inputs are finite; a program needn't handle non-finite values.
Results may differ from a plain program's by a relative error of at most 0.0091.
Values may be sent and summed in bfloat16 or wider, within the bound.
No kernel may reach another device: no remote copies, remote signals or barrier semaphores. Data moves between devices by JAX's collectives and lax.ppermute only.
A program may use at most 256 MiB of HBM per device.

v0:
```python
import jax
import jax.numpy as jnp
from jax import lax
from jax.sharding import PartitionSpec as P

EPSILON = 1e-05


def collect_weights(
    mixer_gain, in_weight, conv_kernel, out_weight, ffn_gain, gate_weight, up_weight, down_weight
):
    tall = (
        lax.all_gather(mixer_gain, "fsdp", axis=0, tiled=True),
        lax.all_gather(conv_kernel, "fsdp", axis=0, tiled=True),
        lax.all_gather(ffn_gain, "fsdp", axis=0, tiled=True),
        lax.all_gather(in_weight, "fsdp", axis=0, tiled=True),
        lax.all_gather(out_weight, "fsdp", axis=0, tiled=True),
        lax.all_gather(gate_weight, "fsdp", axis=0, tiled=True),
        lax.all_gather(up_weight, "fsdp", axis=0, tiled=True),
        lax.all_gather(down_weight, "fsdp", axis=0, tiled=True),
    )
    whole = (
        lax.all_gather(tall[3], "dp", axis=1, tiled=True),
        lax.all_gather(tall[4], "dp", axis=1, tiled=True),
        lax.all_gather(tall[5], "dp", axis=1, tiled=True),
        lax.all_gather(tall[6], "dp", axis=1, tiled=True),
        lax.all_gather(tall[7], "dp", axis=1, tiled=True),
    )
    return (tall[0], tall[1], tall[2], whole[0], whole[1], whole[2], whole[3], whole[4])


def spread_grads(
    grad_gain_one, grad_taps, grad_gain_two, grad_in, grad_outw, grad_gate, grad_up, grad_down
):
    rows = (
        lax.psum_scatter(grad_gain_one, "fsdp", scatter_dimension=0, tiled=True),
        lax.psum_scatter(grad_taps, "fsdp", scatter_dimension=0, tiled=True),
        lax.psum_scatter(grad_gain_two, "fsdp", scatter_dimension=0, tiled=True),
        lax.psum_scatter(grad_in, "fsdp", scatter_dimension=0, tiled=True),
        lax.psum_scatter(grad_outw, "fsdp", scatter_dimension=0, tiled=True),
        lax.psum_scatter(grad_gate, "fsdp", scatter_dimension=0, tiled=True),
        lax.psum_scatter(grad_up, "fsdp", scatter_dimension=0, tiled=True),
        lax.psum_scatter(grad_down, "fsdp", scatter_dimension=0, tiled=True),
    )
    parts = (
        lax.psum_scatter(rows[3], "dp", scatter_dimension=1, tiled=True),
        lax.psum_scatter(rows[4], "dp", scatter_dimension=1, tiled=True),
        lax.psum_scatter(rows[5], "dp", scatter_dimension=1, tiled=True),
        lax.psum_scatter(rows[6], "dp", scatter_dimension=1, tiled=True),
        lax.psum_scatter(rows[7], "dp", scatter_dimension=1, tiled=True),
    )
    smalls = lax.psum((rows[0], rows[1], rows[2]), "dp")
    return (smalls[0], parts[0], smalls[1], parts[1], smalls[2], parts[2], parts[3], parts[4])


def shifted(values, steps):
    return jnp.concatenate(
        [jnp.zeros((steps, values.shape[1]), jnp.float32), values[:-steps]], axis=0
    )


def lifted(values, steps):
    return jnp.concatenate(
        [values[steps:], jnp.zeros((steps, values.shape[1]), jnp.float32)], axis=0
    )


def contract_rows(left, right):
    return lax.dot_general(
        left, right, (((0,), (0,)), ((), ())), preferred_element_type=jnp.float32
    )


def contract_last(left, right):
    return lax.dot_general(
        left, right, (((1,), (1,)), ((), ())), preferred_element_type=jnp.float32
    )


def norm_back(grad_normed, values, inverse, gain):
    weighted = grad_normed * gain
    return inverse * (
        weighted - values * inverse * inverse * jnp.mean(weighted * values, axis=1, keepdims=True)
    )


def body(
    tokens,
    segments,
    mixer_gain,
    in_weight,
    conv_kernel,
    out_weight,
    ffn_gain,
    gate_weight,
    up_weight,
    down_weight,
    cotangent,
):
    width = tokens.shape[1]
    gathered = collect_weights(
        mixer_gain,
        in_weight,
        conv_kernel,
        out_weight,
        ffn_gain,
        gate_weight,
        up_weight,
        down_weight,
    )
    gain_one, kernel_full, gain_two, in_full, out_full, gate_full, up_full, down_full = gathered
    inputs = tokens.astype(jnp.float32)
    inverse_one = lax.rsqrt(jnp.mean(inputs * inputs, axis=1, keepdims=True) + EPSILON)
    normed = (inputs * inverse_one * gain_one.astype(jnp.float32)).astype(jnp.bfloat16)
    projected = jnp.dot(normed, in_full, preferred_element_type=jnp.float32)
    b_part = projected[:, :width]
    c_part = projected[:, width : 2 * width]
    x_part = projected[:, 2 * width :]
    gated = b_part * x_part
    seg_ids = segments[0]
    same_one = jnp.concatenate(
        [jnp.zeros((1,), jnp.float32), (seg_ids[1:] == seg_ids[:-1]).astype(jnp.float32)]
    )[:, None]
    same_two = jnp.concatenate(
        [jnp.zeros((2,), jnp.float32), (seg_ids[2:] == seg_ids[:-2]).astype(jnp.float32)]
    )[:, None]
    kernel_taps = kernel_full.astype(jnp.float32)
    back_one = shifted(gated, 1) * same_one
    back_two = shifted(gated, 2) * same_two
    mixed = kernel_taps[:, 0] * gated + kernel_taps[:, 1] * back_one + kernel_taps[:, 2] * back_two
    scaled = (c_part * mixed).astype(jnp.bfloat16)
    hidden = inputs + contract_last(scaled, out_full)
    inverse_two = lax.rsqrt(jnp.mean(hidden * hidden, axis=1, keepdims=True) + EPSILON)
    normed_two = (hidden * inverse_two * gain_two.astype(jnp.float32)).astype(jnp.bfloat16)
    gate_value = jnp.dot(normed_two, gate_full, preferred_element_type=jnp.float32)
    up_value = jnp.dot(normed_two, up_full, preferred_element_type=jnp.float32)
    sigmoid_gate = jax.nn.sigmoid(gate_value)
    silu_gate = gate_value * sigmoid_gate
    activated = (silu_gate * up_value).astype(jnp.bfloat16)
    result = (hidden + contract_last(activated, down_full)).astype(jnp.bfloat16)
    again_weights = collect_weights(
        mixer_gain,
        in_weight,
        conv_kernel,
        out_weight,
        ffn_gain,
        gate_weight,
        up_weight,
        down_weight,
    )
    gain_one_back, kernel_back, gain_two_back, in_back, out_back, gate_back, up_back, down_back = (
        again_weights
    )
    taps_back = kernel_back.astype(jnp.float32)
    grad_out = cotangent.astype(jnp.float32)
    grad_act = jnp.dot(cotangent, down_back, preferred_element_type=jnp.float32)
    grad_down = contract_rows(cotangent, activated)
    grad_gate_value = (
        grad_act * up_value * sigmoid_gate * (1.0 + gate_value * (1.0 - sigmoid_gate))
    ).astype(jnp.bfloat16)
    grad_up_value = (grad_act * silu_gate).astype(jnp.bfloat16)
    grad_gate = contract_rows(normed_two, grad_gate_value)
    grad_up = contract_rows(normed_two, grad_up_value)
    grad_normed_two = contract_last(grad_gate_value, gate_back) + contract_last(
        grad_up_value, up_back
    )
    grad_gain_two = jnp.sum(grad_normed_two * hidden * inverse_two, axis=0)
    grad_hidden = grad_out + norm_back(
        grad_normed_two, hidden, inverse_two, gain_two_back.astype(jnp.float32)
    )
    grad_branch = grad_hidden.astype(jnp.bfloat16)
    grad_outw = contract_rows(grad_branch, scaled)
    grad_scaled = jnp.dot(grad_branch, out_back, preferred_element_type=jnp.float32)
    grad_c = grad_scaled * mixed
    grad_mixed = grad_scaled * c_part
    grad_gated = (
        taps_back[:, 0] * grad_mixed
        + taps_back[:, 1] * lifted(grad_mixed * same_one, 1)
        + taps_back[:, 2] * lifted(grad_mixed * same_two, 2)
    )
    grad_taps = jnp.stack(
        [
            jnp.sum(grad_mixed * gated, axis=0),
            jnp.sum(grad_mixed * back_one, axis=0),
            jnp.sum(grad_mixed * back_two, axis=0),
        ],
        axis=1,
    )
    grad_projected = jnp.concatenate(
        [grad_gated * x_part, grad_c, grad_gated * b_part], axis=1
    ).astype(jnp.bfloat16)
    grad_in = contract_rows(normed, grad_projected)
    grad_normed = contract_last(grad_projected, in_back)
    grad_gain_one = jnp.sum(grad_normed * inputs * inverse_one, axis=0)
    grad_inputs = grad_hidden + norm_back(
        grad_normed, inputs, inverse_one, gain_one_back.astype(jnp.float32)
    )
    shares = spread_grads(
        grad_gain_one, grad_taps, grad_gain_two, grad_in, grad_outw, grad_gate, grad_up, grad_down
    )
    return (
        result,
        grad_inputs,
        shares[0],
        shares[1],
        shares[2],
        shares[3],
        shares[4],
        shares[5],
        shares[6],
        shares[7],
    )


def solution(mesh):
    return jax.shard_map(
        body,
        mesh=mesh,
        in_specs=(
            P(("dp", "fsdp"), None),
            P(("dp", "fsdp"), None),
            P("fsdp"),
            P("fsdp", "dp"),
            P("fsdp", None),
            P("fsdp", "dp"),
            P("fsdp"),
            P("fsdp", "dp"),
            P("fsdp", "dp"),
            P("fsdp", "dp"),
            P(("dp", "fsdp"), None),
        ),
        out_specs=(
            P(("dp", "fsdp"), None),
            P(("dp", "fsdp"), None),
            P("fsdp"),
            P("fsdp", "dp"),
            P("fsdp", None),
            P("fsdp", "dp"),
            P("fsdp"),
            P("fsdp", "dp"),
            P("fsdp", "dp"),
            P("fsdp", "dp"),
        ),
        check_vma=False,
    )
```

profile of v0, /device:TPU:9, one launch (start us, length us, event | category | flops | bytes accessed | tf_op | source)
XLA Modules:
  0.0 1997.6 jit_solution(3330746338955602927)
XLA Ops:
  10.0 45.3 %all-gather.12.cloned.1.call-done = bf16[1024,768]{1,0:T(8,128)(2,1)} async-done(((bf16[128,768]{1,0:T(8,128)(2,1)}), bf16[1024,768]{1,0:T(8,128)(2,1)}) %all-gather.12.cloned.1.call-update) | async-done | bytes 1572880 | tf_op jit(solution)/shard_map/all_gather | solution.py:16
  55.4 26.0 %all_gather.56 = bf16[1024,256]{1,0:T(8,128)(2,1)} all-gather(bf16[128,256]{1,0:T(8,128)(2,1)S(1)} %copy-done.15), channel_id=1, replica_groups=mesh['dp'=4,'fsdp'=8] {'fsdp'}, dimensions={0}, use_global_device_ids=true | all-gather | bytes 589824 | tf_op jit(solution)/shard_map/all_gather | solution.py:17
  81.4 27.6 %all-gather.18.cloned.1.call-done = bf16[1024,1152]{1,0:T(8,128)(2,1)} async-done(((bf16[128,1152]{1,0:T(8,128)(2,1)}), bf16[1024,1152]{1,0:T(8,128)(2,1)}) %all-gather.18.cloned.1.call-update) | async-done | bytes 2359312 | tf_op jit(solution)/shard_map/all_gather | solution.py:18
  109.1 53.1 %all-gather.22.cloned.1.call-done = bf16[1024,1152]{1,0:T(8,128)(2,1)} async-done(((bf16[128,1152]{1,0:T(8,128)(2,1)}), bf16[1024,1152]{1,0:T(8,128)(2,1)}) %all-gather.22.cloned.1.call-update) | async-done | bytes 2359312 | tf_op jit(solution)/shard_map/all_gather | solution.py:19
  162.3 52.6 %all-gather.26.cloned.1.call-done = bf16[1024,1152]{1,0:T(8,128)(2,1)} async-done(((bf16[128,1152]{1,0:T(8,128)(2,1)}), bf16[1024,1152]{1,0:T(8,128)(2,1)}) %all-gather.26.cloned.1.call-update) | async-done | bytes 2359312 | tf_op jit(solution)/shard_map/all_gather | solution.py:20
  227.5 13.1 all-gather.1
  240.7 15.0 all_gather.55
  273.9 13.2 all-gather.16.cloned.1.call-done
  292.0 60.9 %all-gather.20.cloned.1.call-done = bf16[1024,4608]{1,0:T(8,128)(2,1)} async-done(((bf16[1024,1152]{1,0:T(8,128)(2,1)}), bf16[1024,4608]{1,0:T(8,128)(2,1)}) %all-gather.20.cloned.1.call-update) | async-done | bytes 9437200 | tf_op jit(solution)/shard_map/all_gather | solution.py:25
  364.2 54.4 %all-gather.24.cloned.1.call-done = bf16[1024,4608]{1,0:T(8,128)(2,1)} async-done(((bf16[1024,1152]{1,0:T(8,128)(2,1)}), bf16[1024,4608]{1,0:T(8,128)(2,1)}) %all-gather.24.cloned.1.call-update) | async-done | bytes 9437200 | tf_op jit(solution)/shard_map/all_gather | solution.py:26
  429.9 54.5 %all-gather.28.cloned.1.call-done = bf16[1024,4608]{1,0:T(8,128)(2,1)} async-done(((bf16[1024,1152]{1,0:T(8,128)(2,1)}), bf16[1024,4608]{1,0:T(8,128)(2,1)}) %all-gather.28.cloned.1.call-update) | async-done | bytes 9437200 | tf_op jit(solution)/shard_map/all_gather | solution.py:27
  484.5 17.7 multiply_convert_fusion
  582.0 244.4 %reduce-scatter.30.cloned.1.call-done = f32[128,4608]{0,1:T(8,128)} async-done(((f32[1024,4608]{0,1:T(8,128)}), f32[128,4608]{0,1:T(8,128)}) %reduce-scatter.30.cloned.1.call-update) | async-done | bytes 2359312 | tf_op jit(solution)/shard_map/reduce_scatter | solution.py:43
  826.5 92.1 %reduce-scatter.18.cloned.1.call-done = f32[128,1024]{1,0:T(8,128)} async-done(((f32[1024,1024]{1,0:T(8,128)}), f32[128,1024]{1,0:T(8,128)}) %reduce-scatter.18.cloned.1.call-update) | async-done | bytes 524304 | tf_op jit(solution)/shard_map/reduce_scatter | solution.py:40
  918.7 208.9 %reduce-scatter.14.cloned.1.call-done = f32[128,3072]{1,0:T(8,128)} async-done(((f32[1024,3072]{1,0:T(8,128)}), f32[128,3072]{1,0:T(8,128)}) %reduce-scatter.14.cloned.1.call-update) | async-done | bytes 1572880 | tf_op jit(solution)/shard_map/reduce_scatter | solution.py:39
  1127.7 317.2 %reduce-scatter.22.cloned.1.call-done = f32[128,4608]{1,0:T(8,128)} async-done(((f32[1024,4608]{1,0:T(8,128)}), f32[128,4608]{1,0:T(8,128)}) %reduce-scatter.22.cloned.1.call-update) | async-done | bytes 2359312 | tf_op jit(solution)/shard_map/reduce_scatter | solution.py:41
  1445.0 316.0 %reduce-scatter.26.cloned.1.call-done = f32[128,4608]{1,0:T(8,128)} async-done(((f32[1024,4608]{1,0:T(8,128)}), f32[128,4608]{1,0:T(8,128)}) %reduce-scatter.26.cloned.1.call-update) | async-done | bytes 2359312 | tf_op jit(solution)/shard_map/reduce_scatter | solution.py:42
  1771.2 15.7 all-reduce.7
  1800.7 25.0 %reduce-scatter.34.cloned.1.call-done = f32[128,3]{1,0:T(8,128)} async-done(((f32[1024,3]{1,0:T(8,128)}), f32[128,3]{1,0:T(8,128)}) %reduce-scatter.34.cloned.1.call-update) | async-done | bytes 1552
  1834.8 27.5 %reduce-scatter.32.cloned.1.call-done = f32[128,1152]{0,1:T(8,128)} async-done(((f32[128,4608]{0,1:T(8,128)}), f32[128,1152]{0,1:T(8,128)}) %reduce-scatter.32.cloned.1.call-update) | async-done | bytes 589840 | tf_op jit(solution)/shard_map/reduce_scatter | solution.py:50
  1864.4 22.6 %reduce-scatter.20.cloned.1.call-done = f32[128,256]{1,0:T(8,128)} async-done(((f32[128,1024]{1,0:T(8,128)}), f32[128,256]{1,0:T(8,128)}) %reduce-scatter.20.cloned.1.call-update) | async-done | bytes 131088 | tf_op jit(solution)/shard_map/reduce_scatter | solution.py:47
  1887.0 31.2 %reduce-scatter.16.cloned.1.call-done = f32[128,768]{1,0:T(8,128)} async-done(((f32[128,3072]{1,0:T(8,128)}), f32[128,768]{1,0:T(8,128)}) %reduce-scatter.16.cloned.1.call-update) | async-done | bytes 393232 | tf_op jit(solution)/shard_map/reduce_scatter | solution.py:46
  1918.2 36.3 %reduce-scatter.24.cloned.1.call-done = f32[128,1152]{1,0:T(8,128)} async-done(((f32[128,4608]{1,0:T(8,128)}), f32[128,1152]{1,0:T(8,128)}) %reduce-scatter.24.cloned.1.call-update) | async-done | bytes 589840 | tf_op jit(solution)/shard_map/reduce_scatter | solution.py:48
  1954.6 36.0 %reduce-scatter.28.cloned.1.call-done = f32[128,1152]{1,0:T(8,128)} async-done(((f32[128,4608]{1,0:T(8,128)}), f32[128,1152]{1,0:T(8,128)}) %reduce-scatter.28.cloned.1.call-update) | async-done | bytes 589840 | tf_op jit(solution)/shard_map/reduce_scatter | solution.py:49
  (128 shorter events, 175.5 us)
Async XLA Ops:
  7.2 48.1 %all-gather.12.cloned.1.call-start = ((), (), s32[]{:S(2)}) async-start(), calls=%async_computation.11 | async-start | bytes 1769472 | tf_op jit(solution)/shard_map/all_gather | solution.py:16
  7.9 101.1 %all-gather.18.cloned.1.call-start = ((), (), s32[]{:S(2)}) async-start(), calls=%async_computation.14 | async-start | bytes 2654208 | tf_op jit(solution)/shard_map/all_gather | solution.py:18
  8.7 153.6 %all-gather.22.cloned.1.call-start = ((), (), s32[]{:S(2)}) async-start(), calls=%async_computation.16 | async-start | bytes 2654208 | tf_op jit(solution)/shard_map/all_gather | solution.py:19
  9.4 205.5 %all-gather.26.cloned.1.call-start = ((), (), s32[]{:S(2)}) async-start(), calls=%async_computation.18 | async-start | bytes 2654208 | tf_op jit(solution)/shard_map/all_gather | solution.py:20
  10.0 252.8 %all-gather.14.cloned.1.call-start = ((), (), s32[]{:S(2)}) async-start(), calls=%async_computation.12 | async-start | bytes 7864320 | tf_op jit(solution)/shard_map/all_gather | solution.py:23
  55.3 231.7 %all-gather.16.cloned.1.call-start = ((), (), s32[]{:S(2)}) async-start(), calls=%async_computation.13 | async-start | bytes 2621440 | tf_op jit(solution)/shard_map/all_gather | solution.py:24
  81.4 271.5 %all-gather.20.cloned.1.call-start = ((), (), s32[]{:S(2)}) async-start(), calls=%async_computation.15 | async-start | bytes 11796480 | tf_op jit(solution)/shard_map/all_gather | solution.py:25
  109.1 309.6 %all-gather.24.cloned.1.call-start = ((), (), s32[]{:S(2)}) async-start(), calls=%async_computation.17 | async-start | bytes 11796480 | tf_op jit(solution)/shard_map/all_gather | solution.py:26
  162.2 93.4 %copy-start.16 = (s32[1,512]{1,0:T(1,128)S(1)}, s32[1,512]{1,0:T(1,128)}, u32[]{:S(2)}) copy-start(s32[1,512]{1,0:T(1,128)} %param.12) | copy-start | bytes 6148
  162.2 93.7 %copy-start.3 = (bf16[512,1024]{1,0:T(8,128)(2,1)S(1)}, bf16[512,1024]{1,0:T(8,128)(2,1)}, u32[]{:S(2)}) copy-start(bf16[512,1024]{1,0:T(8,128)(2,1)} %param.11) | copy-start | bytes 3145732
  162.3 322.2 %all-gather.28.cloned.1.call-start = ((), (), s32[]{:S(2)}) async-start(), calls=%async_computation.19 | async-start | bytes 11796480 | tf_op jit(solution)/shard_map/all_gather | solution.py:27
  214.9 611.5 %reduce-scatter.30.cloned.1.call-start = ((), (), s32[]{:S(2)}) async-start(), calls=%async_computation.28 | async-start | bytes 21233664 | tf_op jit(solution)/shard_map/reduce_scatter | solution.py:43
  514.0 404.7 %reduce-scatter.18.cloned.1.call-start = ((), (), s32[]{:S(2)}) async-start(), calls=%async_computation.22 | async-start | bytes 4718592 | tf_op jit(solution)/shard_map/reduce_scatter | solution.py:40
  538.2 589.4 %reduce-scatter.14.cloned.1.call-start = ((), (), s32[]{:S(2)}) async-start(), calls=%async_computation.20 | async-start | bytes 14155776 | tf_op jit(solution)/shard_map/reduce_scatter | solution.py:39
  557.4 887.5 %reduce-scatter.22.cloned.1.call-start = ((), (), s32[]{:S(2)}) async-start(), calls=%async_computation.24 | async-start | bytes 21233664 | tf_op jit(solution)/shard_map/reduce_scatter | solution.py:41
  569.3 1191.8 %reduce-scatter.26.cloned.1.call-start = ((), (), s32[]{:S(2)}) async-start(), calls=%async_computation.26 | async-start | bytes 21233664 | tf_op jit(solution)/shard_map/reduce_scatter | solution.py:42
  580.8 1244.9 %reduce-scatter.34.cloned.1.call-start = ((), (), s32[]{:S(2)}) async-start(), calls=%async_computation.30 | async-start | bytes 589824
  582.0 1280.3 %reduce-scatter.32.cloned.1.call-start = ((), (), s32[]{:S(2)}) async-start(), calls=%async_computation.29 | async-start | bytes 2949120 | tf_op jit(solution)/shard_map/reduce_scatter | solution.py:50
  826.5 1060.5 %reduce-scatter.20.cloned.1.call-start = ((), (), s32[]{:S(2)}) async-start(), calls=%async_computation.23 | async-start | bytes 655360 | tf_op jit(solution)/shard_map/reduce_scatter | solution.py:47
  918.7 999.5 %reduce-scatter.16.cloned.1.call-start = ((), (), s32[]{:S(2)}) async-start(), calls=%async_computation.21 | async-start | bytes 1966080 | tf_op jit(solution)/shard_map/reduce_scatter | solution.py:46
  1127.7 826.9 %reduce-scatter.24.cloned.1.call-start = ((), (), s32[]{:S(2)}) async-start(), calls=%async_computation.25 | async-start | bytes 2949120 | tf_op jit(solution)/shard_map/reduce_scatter | solution.py:48
  1444.9 316.1 %copy-start.20 = (u32[32]{0:T(128)S(1)}, u32[32]{0:T(128)}, u32[]{:S(2)}) copy-start(u32[32]{0:T(128)} %constant.33) | copy-start | bytes 388
  1444.9 317.4 %copy-start.5 = (bf16[512,1024]{1,0:T(8,128)(2,1)S(1)}, bf16[512,1024]{1,0:T(8,128)(2,1)}, u32[]{:S(2)}) copy-start(bf16[512,1024]{1,0:T(8,128)(2,1)} %param.11) | copy-start | bytes 3145732
  1445.0 545.7 %reduce-scatter.28.cloned.1.call-start = ((), (), s32[]{:S(2)}) async-start(), calls=%async_computation.27 | async-start | bytes 2949120 | tf_op jit(solution)/shard_map/reduce_scatter | solution.py:49
  (17 other events, 329.0 us)
Sparse Core Ops, SparseCore 0:
  10.2 45.0 all-gather.11
  57.5 51.4 all-gather.17
  111.2 50.9 all-gather.21
  164.3 50.6 all-gather.25
  216.3 46.3 all-gather.13
  264.2 22.8 all-gather.15
  288.6 64.1 all-gather.19
  354.4 64.1 all-gather.23
  420.2 64.1 all-gather.27
  514.1 312.3 reduce-scatter.29
  830.1 88.4 reduce-scatter.17
  922.5 205.0 reduce-scatter.13
  1132.0 312.8 reduce-scatter.21
  1449.2 311.8 reduce-scatter.25
  1765.2 60.5 reduce-scatter.33
  1828.1 34.1 reduce-scatter.31
  1865.3 21.6 reduce-scatter.19
  1890.0 28.1 reduce-scatter.15
  1921.5 33.0 reduce-scatter.23
  1957.5 33.0 reduce-scatter.27
where the time goes:
time: 2010 us; the launch traced here: 2000 us
  waiting for transfers between devices  1730 us (86%)
  matrix products  138 us (7%)
  blocking collectives  90.5 us (5%)
    reduce_scatter x1, waiting for transfers between devices, spread_grads(): lax.psum_scatter(grad_gate, 'fsdp', scatter_dimension=0, tiled=True)  317 us
    reduce_scatter x1, waiting for transfers between devices, spread_grads(): lax.psum_scatter(grad_up, 'fsdp', scatter_dimension=0, tiled=True)  316 us
    reduce_scatter x1, waiting for transfers between devices, spread_grads(): lax.psum_scatter(grad_down, 'fsdp', scatter_dimension=0, tiled=True)  244 us
    reduce_scatter x1, waiting for transfers between devices, spread_grads(): lax.psum_scatter(grad_in, 'fsdp', scatter_dimension=0, tiled=True)  209 us
    reduce_scatter x1, waiting for transfers between devices, spread_grads(): lax.psum_scatter(grad_outw, 'fsdp', scatter_dimension=0, tiled=True)  92.1 us
    all_gather x1, waiting for transfers between devices, collect_weights(): lax.all_gather(tall[5], 'dp', axis=1, tiled=True)  60.9 us
    all_gather x1, waiting for transfers between devices, collect_weights(): lax.all_gather(tall[7], 'dp', axis=1, tiled=True)  54.5 us
    all_gather x1, waiting for transfers between devices, collect_weights(): lax.all_gather(tall[6], 'dp', axis=1, tiled=True)  54.4 us
  transfers between devices with their start and end apart: 20, of which 20 were waited for; matrix products, arithmetic and copies ran while one was open for 6% of the time, Pallas kernels for 0%

commit v1 on v0

v1 whole, which is shorter than its diff:
```python
import jax
import jax.numpy as jnp
from jax import lax
from jax.sharding import PartitionSpec as P

EPSILON = 1e-05
LINK = jnp.bfloat16
PAD = 128


def dot_plain(left, right):
    return jnp.dot(left, right, preferred_element_type=jnp.float32)


def dot_rows(left, right):
    return lax.dot_general(
        left, right, (((0,), (0,)), ((), ())), preferred_element_type=jnp.float32
    )


def dot_last(left, right):
    return lax.dot_general(
        left, right, (((1,), (1,)), ((), ())), preferred_element_type=jnp.float32
    )


def norm_back(grad_normed, values, inverse, gain):
    weighted = grad_normed * gain
    return inverse * (
        weighted - values * inverse * inverse * jnp.mean(weighted * values, axis=1, keepdims=True)
    )


def shifted(values, steps):
    return jnp.concatenate(
        [jnp.zeros((steps, values.shape[1]), jnp.float32), values[:-steps]], axis=0
    )


def lifted(values, steps):
    return jnp.concatenate(
        [values[steps:], jnp.zeros((steps, values.shape[1]), jnp.float32)], axis=0
    )


def body(
    tokens,
    segments,
    mixer_gain,
    in_weight,
    conv_kernel,
    out_weight,
    ffn_gain,
    gate_weight,
    up_weight,
    down_weight,
    cotangent,
):
    count, width = tokens.shape
    rows = in_weight.shape[0]
    in_cols, out_cols = in_weight.shape[1], out_weight.shape[1]
    ways = width // rows
    half = ways // 2
    place = lax.axis_index("dp")
    low_bit = lax.rem(lax.axis_index("fsdp"), 2)
    low_is_zero = low_bit == 0
    columns = lax.axis_size("dp")
    strides = [[2 * high + low for high in range(half)] for low in range(2)]

    def swap_row(v):
        return lax.ppermute(v, "fsdp", [(i, i ^ 1) for i in range(ways)])

    def swap_far(v):
        return lax.ppermute(v, "dp", [(i, i ^ 2) for i in range(columns)])

    def swap_core(v):
        return lax.ppermute(v, "dp", [(i, i ^ 1) for i in range(columns)])

    def gather_high(v):
        return lax.all_gather(v, "fsdp", axis=0, tiled=True, axis_index_groups=strides)

    def scatter_high(v):
        return lax.psum_scatter(
            v, "fsdp", scatter_dimension=0, tiled=True, axis_index_groups=strides
        )

    def to_own(v):
        parts = v.reshape(v.shape[0], half, 2, rows)
        near = jnp.where(low_is_zero, parts[:, :, 0], parts[:, :, 1])
        away = jnp.where(low_is_zero, parts[:, :, 1], parts[:, :, 0])
        return jnp.concatenate(
            [near.reshape(v.shape[0], -1), away.reshape(v.shape[0], -1)], axis=1
        )

    def from_own(v):
        near = v[:, : width // 2].reshape(v.shape[0], half, rows)
        away = v[:, width // 2 :].reshape(v.shape[0], half, rows)
        zero = jnp.where(low_is_zero, near, away)
        one = jnp.where(low_is_zero, away, near)
        return jnp.stack([zero, one], axis=2).reshape(v.shape[0], width)

    def rows_to_own(v):
        parts = v.reshape(half, 2, rows, v.shape[1])
        near = jnp.where(low_is_zero, parts[:, 0], parts[:, 1])
        away = jnp.where(low_is_zero, parts[:, 1], parts[:, 0])
        return near.reshape(-1, v.shape[1]), away.reshape(-1, v.shape[1])

    def rows_from_own(near, away):
        near = near.reshape(half, rows, -1)
        away = away.reshape(half, rows, -1)
        zero = jnp.where(low_is_zero, near, away)
        one = jnp.where(low_is_zero, away, near)
        return jnp.stack([zero, one], axis=1).reshape(width, -1)

    small = jnp.concatenate(
        [mixer_gain[:, None], ffn_gain[:, None], conv_kernel, jnp.zeros((rows, PAD - 5), LINK)],
        axis=1,
    )
    in_half, out_half = in_cols // 2, out_cols // 2
    packed = jnp.concatenate(
        [
            in_weight[:, :in_half],
            out_weight[:, :out_half],
            small,
            in_weight[:, in_half:],
            out_weight[:, out_half:],
        ],
        axis=1,
    )
    tall = gather_high(packed)
    cut = in_half + out_half
    first = tall[:, : cut + PAD]
    second = tall[:, cut + PAD :]
    first_row = swap_row(first)
    second_far = swap_far(second)
    first_all = jnp.concatenate([first[:, :cut], first_row[:, :cut]], axis=0)
    small_near, small_away = first[:, cut:], first_row[:, cut:]
    second_all = jnp.concatenate([second, second_far], axis=1)
    first_far = swap_far(first_all)
    second_row = swap_row(second_all)
    chip = jnp.concatenate(
        [
            first_all,
            first_far,
            jnp.concatenate([second_all, second_row], axis=0),
        ],
        axis=1,
    )
    chip_core = swap_core(chip)

    def blocks(v):
        ins = [
            jnp.concatenate(
                [v[:, k * cut : k * cut + in_half], v[:, (2 + k) * cut : (2 + k) * cut + in_half]],
                axis=1,
            )
            for k in range(2)
        ]
        outs = [
            jnp.concatenate(
                [
                    v[:, k * cut + in_half : (k + 1) * cut],
                    v[:, (2 + k) * cut + in_half : (3 + k) * cut],
                ],
                axis=1,
            )
            for k in range(2)
        ]
        return ins, outs

    ins_a, outs_a = blocks(chip)
    ins_b, outs_b = blocks(chip_core)
    in_blocks = [ins_a[0], ins_b[0], ins_a[1], ins_b[1]]
    out_rel = jnp.concatenate([outs_a[0], outs_b[0], outs_a[1], outs_b[1]], axis=1)

    def collect(w):
        near = gather_high(w)
        return jnp.concatenate([near, swap_row(near)], axis=0)

    gate_all = collect(gate_weight)
    up_all = collect(up_weight)
    down_all = collect(down_weight)

    def gather_tokens(v):
        far = swap_far(v)
        return jnp.concatenate([v, swap_core(v), far, swap_core(far)], axis=0)

    def sum_tokens(v):
        parts = v.reshape(4, count, width)
        got = swap_core(jnp.concatenate([parts[1], parts[3]], axis=0).astype(LINK))
        far = parts[2] + got[count:].astype(jnp.float32)
        got_far = swap_far(far.astype(LINK))
        return parts[0] + got[:count].astype(jnp.float32) + got_far.astype(jnp.float32)

    def relative(v, size):
        parts = [
            lax.dynamic_slice_in_dim(v, lax.bitwise_xor(place, r) * size, size, 1)
            for r in range(4)
        ]
        return parts

    inputs = to_own(tokens).astype(jnp.float32)
    cot = to_own(cotangent)
    cot_all = gather_tokens(cot)
    small_full = jnp.concatenate([small_near[:, :2], small_away[:, :2]], axis=0).astype(
        jnp.float32
    )
    gain_one = small_full[:, 0]
    gain_two = small_full[:, 1]
    taps = rows_from_own(small_near[:, 2:5], small_away[:, 2:5]).astype(jnp.float32)
    inverse_one = lax.rsqrt(jnp.mean(inputs * inputs, axis=1, keepdims=True) + EPSILON)
    normed = (inputs * inverse_one * gain_one).astype(jnp.bfloat16)
    projected_rel = jnp.stack([dot_plain(normed, w) for w in in_blocks])
    projected = jnp.concatenate(
        [
            lax.dynamic_index_in_dim(projected_rel, lax.bitwise_xor(place, j), 0, False)
            for j in range(4)
        ],
        axis=1,
    )
    b_part = projected[:, :width]
    c_part = projected[:, width : 2 * width]
    x_part = projected[:, 2 * width :]
    gated = b_part * x_part
    seg_ids = segments[0]
    same_one = jnp.concatenate(
        [jnp.zeros((1,), jnp.float32), (seg_ids[1:] == seg_ids[:-1]).astype(jnp.float32)]
    )[:, None]
    same_two = jnp.concatenate(
        [jnp.zeros((2,), jnp.float32), (seg_ids[2:] == seg_ids[:-2]).astype(jnp.float32)]
    )[:, None]
    back_one = shifted(gated, 1) * same_one
    back_two = shifted(gated, 2) * same_two
    mixed = taps[:, 0] * gated + taps[:, 1] * back_one + taps[:, 2] * back_two
    scaled = (c_part * mixed).astype(jnp.bfloat16)
    scaled_rel = jnp.concatenate(relative(scaled, out_cols), axis=1)
    hidden = inputs + dot_last(scaled_rel, out_rel)

    inverse_two = lax.rsqrt(jnp.mean(hidden * hidden, axis=1, keepdims=True) + EPSILON)
    normed_two = gather_tokens((hidden * inverse_two * gain_two).astype(jnp.bfloat16))
    gate_value = dot_plain(normed_two, gate_all)
    up_value = dot_plain(normed_two, up_all)
    sigmoid_gate = jax.nn.sigmoid(gate_value)
    silu_gate = gate_value * sigmoid_gate
    activated = (silu_gate * up_value).astype(jnp.bfloat16)

    def spread(left, right):
        away = dot_rows(left[:, width // 2 :], right).astype(LINK)
        near = dot_rows(left[:, : width // 2], right)
        total = near + swap_row(away).astype(jnp.float32)
        return scatter_high(total.astype(LINK)).astype(jnp.float32)

    grad_down = spread(cot_all, activated)
    grad_act = dot_plain(cot_all, down_all)
    grad_gate_value = (
        grad_act * up_value * sigmoid_gate * (1.0 + gate_value * (1.0 - sigmoid_gate))
    ).astype(jnp.bfloat16)
    grad_up_value = (grad_act * silu_gate).astype(jnp.bfloat16)
    grad_normed_two = sum_tokens(
        dot_last(grad_gate_value, gate_all) + dot_last(grad_up_value, up_all)
    )
    grad_gate = spread(normed_two, grad_gate_value)
    grad_up = spread(normed_two, grad_up_value)
    result = from_own(hidden + sum_tokens(dot_last(activated, down_all))).astype(jnp.bfloat16)

    grad_gain_two = jnp.sum(grad_normed_two * hidden * inverse_two, axis=0)
    grad_hidden = cot.astype(jnp.float32) + norm_back(
        grad_normed_two, hidden, inverse_two, gain_two
    )
    grad_branch = grad_hidden.astype(jnp.bfloat16)
    grad_outw_rel = dot_rows(grad_branch, scaled_rel)
    grad_scaled_rel = dot_plain(grad_branch, out_rel)
    grad_scaled = jnp.concatenate(relative(grad_scaled_rel, out_cols), axis=1)
    grad_c = grad_scaled * mixed
    grad_mixed = grad_scaled * c_part
    grad_gated = (
        taps[:, 0] * grad_mixed
        + taps[:, 1] * lifted(grad_mixed * same_one, 1)
        + taps[:, 2] * lifted(grad_mixed * same_two, 2)
    )
    grad_taps = jnp.stack(
        [
            jnp.sum(grad_mixed * gated, axis=0),
            jnp.sum(grad_mixed * back_one, axis=0),
            jnp.sum(grad_mixed * back_two, axis=0),
        ],
        axis=1,
    )
    grad_projected = jnp.concatenate(
        [grad_gated * x_part, grad_c, grad_gated * b_part], axis=1
    ).astype(jnp.bfloat16)
    grad_proj_rel = relative(grad_projected, in_cols)
    grad_normed = (
        dot_last(grad_proj_rel[0], in_blocks[0])
        + dot_last(grad_proj_rel[1], in_blocks[1])
        + dot_last(grad_proj_rel[2], in_blocks[2])
        + dot_last(grad_proj_rel[3], in_blocks[3])
    )
    grad_gain_one = jnp.sum(grad_normed * inputs * inverse_one, axis=0)
    grad_inputs = from_own(
        grad_hidden + norm_back(grad_normed, inputs, inverse_one, gain_one)
    )

    grad_in_rel = [dot_rows(normed, g) for g in grad_proj_rel]
    taps_near, taps_away = rows_to_own(grad_taps)
    small_grad = jnp.concatenate(
        [
            grad_gain_one[:, None],
            grad_gain_two[:, None],
            jnp.concatenate([taps_near, taps_away], axis=0),
            jnp.zeros((width, PAD - 5), jnp.float32),
        ],
        axis=1,
    )

    def pack(ins, outs):
        return jnp.concatenate(
            [
                piece
                for lo, hi, lo2, hi2 in ((0, in_half, 0, out_half), (in_half, in_cols, out_half, out_cols))
                for k in range(2)
                for piece in (ins[k][:, lo:hi], outs[k][:, lo2:hi2])
            ],
            axis=1,
        )

    def out_block(r):
        return grad_outw_rel[:, r * out_cols : (r + 1) * out_cols]

    mine = pack([grad_in_rel[0], grad_in_rel[2]], [out_block(0), out_block(2)])
    other = pack([grad_in_rel[1], grad_in_rel[3]], [out_block(1), out_block(3)])
    got = swap_core(jnp.concatenate([other, small_grad], axis=1).astype(LINK)).astype(jnp.float32)
    mine = mine + got[:, : 4 * cut]
    small_sum = small_grad + got[:, 4 * cut :]
    first_own = jnp.concatenate([mine[:, :cut], small_sum], axis=1)
    got_first = swap_far(jnp.concatenate([mine[:, cut : 2 * cut], small_sum], axis=1).astype(LINK))
    first_own = first_own + got_first.astype(jnp.float32)
    got_first = swap_row(first_own[width // 2 :].astype(LINK))
    first_done = first_own[: width // 2] + got_first.astype(jnp.float32)
    got_second = swap_row(mine[width // 2 :, 2 * cut :].astype(LINK))
    second_own = mine[: width // 2, 2 * cut :] + got_second.astype(jnp.float32)
    got_second = swap_far(second_own[:, cut:].astype(LINK))
    second_done = second_own[:, :cut] + got_second.astype(jnp.float32)
    owned = scatter_high(
        jnp.concatenate([first_done, second_done], axis=1).astype(LINK)
    ).astype(jnp.float32)
    grad_in = jnp.concatenate(
        [owned[:, :in_half], owned[:, cut + PAD : cut + PAD + in_half]], axis=1
    )
    grad_outw = jnp.concatenate(
        [owned[:, in_half:cut], owned[:, cut + PAD + in_half :]], axis=1
    )
    return (
        result,
        grad_inputs,
        owned[:, cut],
        grad_in,
        owned[:, cut + 2 : cut + 5],
        grad_outw,
        owned[:, cut + 1],
        grad_gate,
        grad_up,
        grad_down,
    )


def solution(mesh):
    return jax.shard_map(
        body,
        mesh=mesh,
        in_specs=(
            P(("dp", "fsdp"), None),
            P(("dp", "fsdp"), None),
            P("fsdp"),
            P("fsdp", "dp"),
            P("fsdp", None),
            P("fsdp", "dp"),
            P("fsdp"),
            P("fsdp", "dp"),
            P("fsdp", "dp"),
            P("fsdp", "dp"),
            P(("dp", "fsdp"), None),
        ),
        out_specs=(
            P(("dp", "fsdp"), None),
            P(("dp", "fsdp"), None),
            P("fsdp"),
            P("fsdp", "dp"),
            P("fsdp", None),
            P("fsdp", "dp"),
            P("fsdp"),
            P("fsdp", "dp"),
            P("fsdp", "dp"),
            P("fsdp", "dp"),
        ),
        check_vma=False,
    )
```

time: 2010 us -> 557 us (0.28)
  the two profiles are of different devices: /device:TPU:9 before, /device:TPU:0 now
where the time goes in v1:
time: 557 us; the launch traced here: 547 us
  waiting for transfers between devices  162 us (29%)
  matrix products  132 us (24%)
  local copies, waits for them, and re-layouts  128 us (23%)
  other arithmetic  88.2 us (16%)
  starting transfers between devices  20.1 us (4%)
  between operations  15.9 us (3%)
    ppermute x10, waiting for transfers between devices, swap_row(): return lax.ppermute(v, 'fsdp', [(i, i ^ 1) for i in range(ways)])  64 us
    ppermute x8, waiting for transfers between devices, swap_far(): return lax.ppermute(v, 'dp', [(i, i ^ 2) for i in range(columns)])  51.5 us
    dot_general x8, matrix products, dot_plain(): return jnp.dot(left, right, preferred_element_type=jnp.float32)  47.8 us
    all_gather x4, waiting for transfers between devices, gather_high(): lax.all_gather(v, 'fsdp', axis=0, tiled=True, axis_index_groups=strides)  45.3 us
    unnamed x190, local copies, waits for them, and re-layouts  45.1 us
    dot_general x11, matrix products, dot_rows(): lax.dot_general(left, right, (((0,), (0,)), ((), ())), preferred_element_...  44.7 us
    dot_general x8, matrix products, dot_last(): lax.dot_general(left, right, (((1,), (1,)), ((), ())), preferred_element_...  39.3 us
    concatenate x1, local copies, waits for them, and re-layouts, body(): jnp.concatenate([other, small_grad], axis=1).astype(LINK)  26 us
  transfers between devices with their start and end apart: 34, of which 16 were waited for; matrix products, arithmetic and copies ran while one was open for 48% of the time, Pallas kernels for 0%

profile of v1, /device:TPU:0, one launch (start us, length us, event | category | flops | bytes accessed | tf_op | source)
XLA Modules:
  0.0 546.7 jit_solution(10141136841604882521)
XLA Ops:
  16.3 33.1 %all-gather.5.cloned.1.call-done = bf16[512,1152]{0,1:T(8,128)(2,1)} async-done(((bf16[128,1152]{0,1:T(8,128)(2,1)}), bf16[512,1152]{0,1:T(8,128)(2,1)}) %all-gather.5.cloned.1.call-update) | async-done | bytes 1179664 | tf_op jit(solution)/shard_map/all_gather | solution.py:80
  53.4 10.6 %collective-permute-done.1 = bf16[512,512]{0,1:T(8,128)(2,1)S(1)} collective-permute-done((bf16[512,512]{0,1:T(8,128)(2,1)S(1)}, bf16[512,512]{0,1:T(8,128)(2,1)S(1)}, u32[]{:S(2)}, u32[]{:S(2)}) %collective-permute-start.1) | collective-permute-done | bytes 524320 | tf_op jit(solution)/shard_map/ppermute | solution.py:74
  81.1 9.7 %collective-permute-done.2 = bf16[512,1024]{0,1:T(8,128)(2,1)S(1)} collective-permute-done((bf16[512,1024]{0,1:T(8,128)(2,1)}, bf16[512,1024]{0,1:T(8,128)(2,1)S(1)}, u32[]{:S(2)}, u32[]{:S(2)}) %collective-permute-start.2) | collective-permute-done | bytes 1048608 | tf_op jit(solution)/shard_map/ppermute | solution.py:71
  94.7 16.5 %maximum_maximum_fusion = bf16[1024,2048]{0,1:T(8,128)(2,1)} fusion(bf16[512,1024]{0,1:T(8,128)(2,1)S(1)} %collective-permute-done.2, bf16[512,512]{0,1:T(8,128)(2,1)S(1)} %collective-permute-done.1, bf16[512,512]{0,1:T(8,128)(2,1)S(1)} %get-tuple-element.96, bf16[1024,512]{0,1:T(8,128)(2,1)} %collective-permute-done.3, bf16[512,512]{0,1:T(8,128)(2,1)S(1)} %slice.481, ...), kind=kLoop, calls=%fused_computation.7 | loop fusion | flops 25165824 | bytes 8388608 | tf_op jit(solution)/shard_map/concatenate | solution.py:141
  129.8 12.2 %all-gather.7.cloned.1.call-done = bf16[512,1152]{1,0:T(8,128)(2,1)} async-done(((bf16[128,1152]{1,0:T(8,128)(2,1)}), bf16[512,1152]{1,0:T(8,128)(2,1)}) %all-gather.7.cloned.1.call-update) | async-done | bytes 1179664 | tf_op jit(solution)/shard_map/all_gather | solution.py:80
  173.7 8.4 %collective-permute-done.10 = bf16[512,1152]{1,0:T(8,128)(2,1)} collective-permute-done((bf16[512,1152]{1,0:T(8,128)(2,1)}, bf16[512,1152]{1,0:T(8,128)(2,1)}, u32[]{:S(2)}, u32[]{:S(2)}) %collective-permute-start.10) | collective-permute-done | bytes 1179680 | tf_op jit(solution)/shard_map/ppermute | solution.py:71
  183.7 9.9 %collective-permute-done.6 = bf16[512,1024]{1,0:T(8,128)(2,1)S(1)} collective-permute-done((bf16[512,1024]{1,0:T(8,128)(2,1)S(1)}, bf16[512,1024]{1,0:T(8,128)(2,1)S(1)}, u32[]{:S(2)}, u32[]{:S(2)}) %collective-permute-start.6) | collective-permute-done | bytes 1048608 | tf_op jit(solution)/shard_map/ppermute | solution.py:74
  193.6 13.1 %collective-permute-done.8 = bf16[512,1152]{1,0:T(8,128)(2,1)} collective-permute-done((bf16[512,1152]{1,0:T(8,128)(2,1)}, bf16[512,1152]{1,0:T(8,128)(2,1)}, u32[]{:S(2)}, u32[]{:S(2)}) %collective-permute-start.8) | collective-permute-done | bytes 1179680 | tf_op jit(solution)/shard_map/ppermute | solution.py:71
  209.6 12.5 %fusion.71 = f32[2048,1152]{1,0:T(8,128)} fusion(bf16[1024,1152]{1,0:T(8,128)(2,1)S(1)} %constant_dynamic-update-slice_fusion.4, bf16[512,1024]{1,0:T(8,128)(2,1)S(1)} %collective-permute-done.15, bf16[512,1024]{1,0:T(8,128)(2,1)} %collective-permute-done.14, bf16[512,1024]{1,0:T(8,128)(2,1)S(1)} %collective-permute-done.13, ...), kind=kOutput, calls=%fused_computation.218 | convolution fusion | flops 4848615424 | bytes 15990784 | tf_op jit(solution)/shard_map/dot_general | solution.py:12
  224.0 11.3 %fusion.80 = f32[2048,1152]{1,0:T(8,128)} fusion(bf16[1024,1152]{1,0:T(8,128)(2,1)S(1)} %constant_dynamic-update-slice_fusion.2, bf16[512,1024]{1,0:T(8,128)(2,1)S(1)} %collective-permute-done.7, bf16[512,1024]{1,0:T(8,128)(2,1)S(1)} %collective-permute-done.6, bf16[512,1024]{1,0:T(8,128)(2,1)S(1)} %collective-permute-done.5, ...), kind=kOutput, calls=%fused_computation.219 | convolution fusion | flops 4848615424 | bytes 15990784 | tf_op jit(solution)/shard_map/dot_general | solution.py:12
  235.3 18.6 %multiply_convert_fusion.1 = (bf16[2048,1152]{1,0:T(8,128)(2,1)}, bf16[2048,1152]{1,0:T(8,128)(2,1)}, bf16[2048,1152]{1,0:T(8,128)(2,1)}) fusion(f32[2048,1152]{1,0:T(8,128)} %fusion.71, f32[2048,1152]{1,0:T(8,128)} %fusion.80, bf16[1024,1152]{1,0:T(8,128)(2,1)} %copy-done.68, bf16[512,1024]{1,0:T(8,128)(2,1)} %copy-done.52, ...), kind=kOutput, calls=%fused_computation.1 | convolution fusion | flops 4884004864 | bytes 39583744 | tf_op jit(solution)/shard_map/dot_general | solution.py:12
  254.0 10.9 %fusion.104 = f32[2048,1024]{1,0:T(8,128)} fusion(bf16[2048,1152]{1,0:T(8,128)(2,1)} %get-tuple-element.59, bf16[1024,1152]{1,0:T(8,128)(2,1)} %copy-done.67), kind=kOutput, calls=%fused_computation.242 | convolution fusion | flops 4831838208 | bytes 15466496 | tf_op jit(solution)/shard_map/dot_general | solution.py:22
  264.8 10.9 %fusion.102 = (bf16[2048,1024]{1,0:T(8,128)(2,1)S(1)}, f32[2048,1024]{1,0:T(8,128)S(1)}) fusion(f32[2048,1024]{1,0:T(8,128)} %fusion.104, bf16[2048,1152]{1,0:T(8,128)(2,1)S(1)} %copy-done.79, bf16[1024,1152]{1,0:T(8,128)(2,1)S(1)} %copy-done.69), kind=kOutput, calls=%fused_computation.240 | convolution fusion | flops 4836032512 | bytes 28049408 | tf_op jit(solution)/shard_map/dot_general | solution.py:22
  289.4 7.8 %convolution_convert_fusion.1 = bf16[512,1152]{1,0:T(8,128)(2,1)} fusion(bf16[2048,1152]{1,0:T(8,128)(2,1)} %get-tuple-element.59, bf16[2048,1024]{1,0:T(8,128)(2,1)S(1)} %pad_maximum_fusion.1), kind=kOutput, calls=%fused_computation.24 | convolution fusion | flops 2416508928 | bytes 7995392 | tf_op jit(solution)/shard_map/dot_general | solution.py:16
  306.4 9.6 %collective-permute-done.25 = bf16[512,1152]{1,0:T(8,128)(2,1)S(1)} collective-permute-done((bf16[512,1152]{1,0:T(8,128)(2,1)S(1)}, bf16[512,1152]{1,0:T(8,128)(2,1)S(1)}, u32[]{:S(2)}, u32[]{:S(2)}) %collective-permute-start.25) | collective-permute-done | bytes 1179680 | tf_op jit(solution)/shard_map/ppermute | solution.py:71
  357.1 26.0 %concatenate.173 = bf16[1024,2176]{0,1:T(8,128)(2,1)} concatenate(bf16[1024,384]{0,1:T(8,128)(2,1)} %get-tuple-element.95, bf16[1024,128]{0,1:T(8,128)(2,1)} %get-tuple-element.76, bf16[1024,384]{0,1:T(8,128)(2,1)} %get-tuple-element.93, bf16[1024,128]{0,1:T(8,128)(2,1)} %get-tuple-element.75, bf16[1024,384]{0,1:T(8,128)(2,1)} %get-tuple-element.94, ...), dimensions={1} | concatenate | bytes 8912896 | tf_op jit(solution)/shard_map/concatenate | solution.py:332
  383.1 11.5 %fusion.101 = (bf16[2048,1024]{1,0:T(8,128)(2,1)}, f32[2048,1024]{1,0:T(8,128)}) fusion(bf16[2048,1152]{1,0:T(8,128)(2,1)} %get-tuple-element.60, bf16[1024,1152]{1,0:T(8,128)(2,1)} %copy-done.70), kind=kOutput, calls=%fused_computation.239 | convolution fusion | flops 4833935360 | bytes 19660800 | tf_op jit(solution)/shard_map/dot_general | solution.py:22
  394.6 6.7 %fusion.2 = bf16[512,1152]{1,0:T(8,128)(2,1)} fusion(bf16[2048,1152]{1,0:T(8,128)(2,1)} %get-tuple-element.59, bf16[512,1152]{1,0:T(8,128)(2,1)} %collective-permute-done.24, bf16[2048,1024]{1,0:T(8,128)(2,1)S(1)} %copy-done.27), kind=kOutput, calls=%fused_computation.21 | convolution fusion | flops 2417688576 | bytes 9175040 | tf_op jit(solution)/shard_map/dot_general | solution.py:16
  414.6 6.9 %convert_element_type.158 = f32[1024,2176]{0,1:T(8,128)} convert(bf16[1024,2176]{0,1:T(8,128)(2,1)} %collective-permute-done.18) | non-fusion elementwise | flops 2228224 | bytes 13369344 | tf_op jit(solution)/shard_map/convert_element_type | solution.py:332
  421.5 13.5 %fusion.83 = (bf16[1024,2048]{0,1:T(8,128)(2,1)}, f32[1024,2048]{0,1:T(8,128)}) fusion(f32[1024,2048]{0,1:T(8,128)} %slice_dynamic-update-slice_fusion.4, f32[1024,2176]{0,1:T(8,128)} %convert_element_type.158), kind=kLoop, calls=%fused_computation.222 | loop fusion | flops 4194304 | bytes 29360128 | tf_op jit(solution)/shard_map/convert.14
  455.4 13.4 %collective-permute-done.21 = bf16[512,1024]{0,1:T(8,128)(2,1)} collective-permute-done((bf16[512,1024]{0,1:T(8,128)(2,1)}, bf16[512,1024]{0,1:T(8,128)(2,1)}, u32[]{:S(2)}, u32[]{:S(2)}) %collective-permute-start.21) | collective-permute-done | bytes 1048608 | tf_op jit(solution)/shard_map/ppermute | solution.py:71
  475.5 8.8 %collective-permute-done.22 = bf16[512,512]{0,1:T(8,128)(2,1)S(1)} collective-permute-done((bf16[512,512]{0,1:T(8,128)(2,1)S(1)}, bf16[512,512]{0,1:T(8,128)(2,1)S(1)}, u32[]{:S(2)}, u32[]{:S(2)}) %collective-permute-start.22) | collective-permute-done | bytes 524320 | tf_op jit(solution)/shard_map/ppermute | solution.py:74
  484.5 7.0 %collective-permute-done.20 = bf16[512,640]{0,1:T(8,128)(2,1)S(1)} collective-permute-done((bf16[512,640]{0,1:T(8,128)(2,1)S(1)}, bf16[512,640]{0,1:T(8,128)(2,1)S(1)}, u32[]{:S(2)}, u32[]{:S(2)}) %collective-permute-start.20) | collective-permute-done | bytes 655392 | tf_op jit(solution)/shard_map/ppermute | solution.py:71
  509.4 13.4 %collective-permute-done.12 = bf16[512,1024]{1,0:T(8,128)(2,1)} collective-permute-done((bf16[512,1024]{1,0:T(8,128)(2,1)}, bf16[512,1024]{1,0:T(8,128)(2,1)}, u32[]{:S(2)}, u32[]{:S(2)}) %collective-permute-start.12) | collective-permute-done | bytes 1048608 | tf_op jit(solution)/shard_map/ppermute | solution.py:74
  (395 shorter events, 228.5 us)
Async XLA Ops:
  7.2 42.2 %all-gather.5.cloned.1.call-start = ((), (), s32[]{:S(2)}) async-start(), calls=%async_computation.4 | async-start | bytes 1474560 | tf_op jit(solution)/shard_map/all_gather | solution.py:80
  14.8 112.9 %all-gather.9.cloned.1.call-start = ((), (), s32[]{:S(2)}) async-start(), calls=%async_computation.6 | async-start | bytes 1474560 | tf_op jit(solution)/shard_map/all_gather | solution.py:80
  15.5 114.0 %all-gather.11.cloned.1.call-start = ((), (), s32[]{:S(2)}) async-start(), calls=%async_computation.7 | async-start | bytes 1474560 | tf_op jit(solution)/shard_map/all_gather | solution.py:80
  16.2 125.7 %all-gather.7.cloned.1.call-start = ((), (), s32[]{:S(2)}) async-start(), calls=%async_computation.5 | async-start | bytes 1474560 | tf_op jit(solution)/shard_map/all_gather | solution.py:80
  65.0 25.8 %collective-permute-start.2 = (bf16[512,1024]{0,1:T(8,128)(2,1)}, bf16[512,1024]{0,1:T(8,128)(2,1)S(1)}, u32[]{:S(2)}, u32[]{:S(2)}) collective-permute-start(bf16[512,1024]{0,1:T(8,128)(2,1)} %pad_maximum_fusion.20), channel_id=1, source_target_pairs={{0,1},{1,0},{2,3},{3,2},{4,5},{5,4},{6,7},{7,6},{8,9},{9,8},{10,11... | collective-permute-start | bytes 3145736 | tf_op jit(solution)/shard_map/ppermute | solution.py:71
  71.5 458.4 %reduce-scatter.11.cloned.1.call-start = ((), (), s32[]{:S(2)}) async-start(), calls=%async_computation.10 | async-start | bytes 1474560 | tf_op jit(solution)/shard_map/reduce_scatter | solution.py:83
  111.2 40.1 %collective-permute-start.4 = (bf16[1024,2048]{0,1:T(8,128)(2,1)}, bf16[1024,2048]{0,1:T(8,128)(2,1)}, u32[]{:S(2)}, u32[]{:S(2)}) collective-permute-start(bf16[1024,2048]{0,1:T(8,128)(2,1)} %maximum_maximum_fusion), channel_id=1, source_target_pairs={{0,8},{8,0},{16,24},{24,16},{1,9},{9,1},{17,25},{25,17},{2,10},{10... | collective-permute-start | bytes 12582920 | tf_op jit(solution)/shard_map/ppermute | solution.py:77
  119.9 51.4 %collective-permute-start.14 = (bf16[512,1024]{1,0:T(8,128)(2,1)}, bf16[512,1024]{1,0:T(8,128)(2,1)}, u32[]{:S(2)}, u32[]{:S(2)}) collective-permute-start(bf16[512,1024]{1,0:T(8,128)(2,1)} %bitcast_dynamic-update-slice_fusion), channel_id=1, source_target_pairs={{0,16},{8,24},{16,0},{24,8},{1,17},{9,25},{17,1},{25,9},{2,18},{10... | collective-permute-start | bytes 3145736 | tf_op jit(solution)/shard_map/ppermute | solution.py:74
  127.7 43.7 %collective-permute-start.9 = (bf16[512,1152]{1,0:T(8,128)(2,1)}, bf16[512,1152]{1,0:T(8,128)(2,1)}, u32[]{:S(2)}, u32[]{:S(2)}) collective-permute-start(bf16[512,1152]{1,0:T(8,128)(2,1)} %all-gather.9.cloned.1.call-done), channel_id=1, source_target_pairs={{0,1},{1,0},{2,3},{3,2},{4,5},{5,4},{6,7},{7,6},{8,9},{9,8},{10,11... | collective-permute-start | bytes 3538952 | tf_op jit(solution)/shard_map/ppermute | solution.py:71
  129.5 52.6 %collective-permute-start.10 = (bf16[512,1152]{1,0:T(8,128)(2,1)}, bf16[512,1152]{1,0:T(8,128)(2,1)}, u32[]{:S(2)}, u32[]{:S(2)}) collective-permute-start(bf16[512,1152]{1,0:T(8,128)(2,1)} %all-gather.11.cloned.1.call-done), channel_id=1, source_target_pairs={{0,1},{1,0},{2,3},{3,2},{4,5},{5,4},{6,7},{7,6},{8,9},{9,8},{10,11... | collective-permute-start | bytes 3538952 | tf_op jit(solution)/shard_map/ppermute | solution.py:71
  141.9 64.8 %collective-permute-start.8 = (bf16[512,1152]{1,0:T(8,128)(2,1)}, bf16[512,1152]{1,0:T(8,128)(2,1)}, u32[]{:S(2)}, u32[]{:S(2)}) collective-permute-start(bf16[512,1152]{1,0:T(8,128)(2,1)} %all-gather.7.cloned.1.call-done), channel_id=1, source_target_pairs={{0,1},{1,0},{2,3},{3,2},{4,5},{5,4},{6,7},{7,6},{8,9},{9,8},{10,11... | collective-permute-start | bytes 3538952 | tf_op jit(solution)/shard_map/ppermute | solution.py:71
  171.3 36.9 %collective-permute-start.13 = (bf16[512,1024]{1,0:T(8,128)(2,1)}, bf16[512,1024]{1,0:T(8,128)(2,1)S(1)}, u32[]{:S(2)}, u32[]{:S(2)}) collective-permute-start(bf16[512,1024]{1,0:T(8,128)(2,1)} %bitcast_dynamic-update-slice_fusion), channel_id=1, source_target_pairs={{0,8},{8,0},{16,24},{24,16},{1,9},{9,1},{17,25},{25,17},{2,10},{10... | collective-permute-start | bytes 3145736 | tf_op jit(solution)/shard_map/ppermute | solution.py:77
  171.4 38.2 %collective-permute-start.15 = (bf16[512,1024]{1,0:T(8,128)(2,1)}, bf16[512,1024]{1,0:T(8,128)(2,1)S(1)}, u32[]{:S(2)}, u32[]{:S(2)}) collective-permute-start(bf16[512,1024]{1,0:T(8,128)(2,1)} %collective-permute-done.14), channel_id=1, source_target_pairs={{0,8},{8,0},{16,24},{24,16},{1,9},{9,1},{17,25},{25,17},{2,10},{10... | collective-permute-start | bytes 3145736 | tf_op jit(solution)/shard_map/ppermute | solution.py:77
  183.6 38.5 %collective-permute-start.5 = (bf16[512,1024]{1,0:T(8,128)(2,1)S(1)}, bf16[512,1024]{1,0:T(8,128)(2,1)S(1)}, u32[]{:S(2)}, u32[]{:S(2)}) collective-permute-start(bf16[512,1024]{1,0:T(8,128)(2,1)S(1)} %multiply_convert_fusion.6), channel_id=1, source_target_pairs={{0,8},{8,0},{16,24},{24,16},{1,9},{9,1},{17,25},{25,17},{2,10},{10... | collective-permute-start | bytes 3145736 | tf_op jit(solution)/shard_map/ppermute | solution.py:77
  193.6 28.5 %collective-permute-start.7 = (bf16[512,1024]{1,0:T(8,128)(2,1)S(1)}, bf16[512,1024]{1,0:T(8,128)(2,1)S(1)}, u32[]{:S(2)}, u32[]{:S(2)}) collective-permute-start(bf16[512,1024]{1,0:T(8,128)(2,1)S(1)} %collective-permute-done.6), channel_id=1, source_target_pairs={{0,8},{8,0},{16,24},{24,16},{1,9},{9,1},{17,25},{25,17},{2,10},{10... | collective-permute-start | bytes 3145736 | tf_op jit(solution)/shard_map/ppermute | solution.py:77
  287.0 29.0 %collective-permute-start.25 = (bf16[512,1152]{1,0:T(8,128)(2,1)S(1)}, bf16[512,1152]{1,0:T(8,128)(2,1)S(1)}, u32[]{:S(2)}, u32[]{:S(2)}) collective-permute-start(bf16[512,1152]{1,0:T(8,128)(2,1)S(1)} %convolution_convert_fusion), channel_id=1, source_target_pairs={{0,1},{1,0},{2,3},{3,2},{4,5},{5,4},{6,7},{7,6},{8,9},{9,8},{10,11... | collective-permute-start | bytes 3538952 | tf_op jit(solution)/shard_map/ppermute | solution.py:71
  304.4 90.2 %collective-permute-start.24 = (bf16[512,1152]{1,0:T(8,128)(2,1)}, bf16[512,1152]{1,0:T(8,128)(2,1)}, u32[]{:S(2)}, u32[]{:S(2)}) collective-permute-start(bf16[512,1152]{1,0:T(8,128)(2,1)} %convolution_convert_fusion.1), channel_id=1, source_target_pairs={{0,1},{1,0},{2,3},{3,2},{4,5},{5,4},{6,7},{7,6},{8,9},{9,8},{10,11... | collective-permute-start | bytes 3538952 | tf_op jit(solution)/shard_map/ppermute | solution.py:71
  304.9 138.8 %collective-permute-start.23 = (bf16[512,1152]{1,0:T(8,128)(2,1)}, bf16[512,1152]{1,0:T(8,128)(2,1)}, u32[]{:S(2)}, u32[]{:S(2)}) collective-permute-start(bf16[512,1152]{1,0:T(8,128)(2,1)} %convolution_convert_fusion.2), channel_id=1, source_target_pairs={{0,1},{1,0},{2,3},{3,2},{4,5},{5,4},{6,7},{7,6},{8,9},{9,8},{10,11... | collective-permute-start | bytes 3538952 | tf_op jit(solution)/shard_map/ppermute | solution.py:71
  319.9 211.8 %reduce-scatter.9.cloned.1.call-start = ((), (), s32[]{:S(2)}) async-start(), calls=%async_computation.9 | async-start | bytes 1474560 | tf_op jit(solution)/shard_map/reduce_scatter | solution.py:83
  383.1 31.4 %collective-permute-start.18 = (bf16[1024,2176]{0,1:T(8,128)(2,1)}, bf16[1024,2176]{0,1:T(8,128)(2,1)}, u32[]{:S(2)}, u32[]{:S(2)}) collective-permute-start(bf16[1024,2176]{0,1:T(8,128)(2,1)} %concatenate.173), channel_id=1, source_target_pairs={{0,8},{8,0},{16,24},{24,16},{1,9},{9,1},{17,25},{25,17},{2,10},{10... | collective-permute-start | bytes 13369352 | tf_op jit(solution)/shard_map/ppermute | solution.py:77
  401.4 132.2 %reduce-scatter.7.cloned.1.call-start = ((), (), s32[]{:S(2)}) async-start(), calls=%async_computation.8 | async-start | bytes 1474560 | tf_op jit(solution)/shard_map/reduce_scatter | solution.py:83
  441.9 31.5 %collective-permute-start.19 = (bf16[1024,640]{0,1:T(8,128)(2,1)}, bf16[1024,640]{0,1:T(8,128)(2,1)}, u32[]{:S(2)}, u32[]{:S(2)}) collective-permute-start(bf16[1024,640]{0,1:T(8,128)(2,1)} %pad_maximum_fusion.17), channel_id=1, source_target_pairs={{0,16},{8,24},{16,0},{24,8},{1,17},{9,25},{17,1},{25,9},{2,18},{10... | collective-permute-start | bytes 3932168 | tf_op jit(solution)/shard_map/ppermute | solution.py:74
  450.3 85.0 %reduce-scatter.13.cloned.1.call-start = ((), (), s32[]{:S(2)}) async-start(), calls=%async_computation.11 | async-start | bytes 1474560
  453.6 42.0 %collective-permute-start.11 = (bf16[1024,1024]{1,0:T(8,128)(2,1)}, bf16[1024,1024]{1,0:T(8,128)(2,1)}, u32[]{:S(2)}, u32[]{:S(2)}) collective-permute-start(bf16[1024,1024]{1,0:T(8,128)(2,1)} %pad_maximum_fusion.8), channel_id=1, source_target_pairs={{0,8},{8,0},{16,24},{24,16},{1,9},{9,1},{17,25},{25,17},{2,10},{10... | collective-permute-start | bytes 6291464 | tf_op jit(solution)/shard_map/ppermute | solution.py:77
  (94 other events, 795.2 us)
Sparse Core Ops, SparseCore 0:
  14.9 34.4 all-gather.4
  50.9 28.7 all-gather.8
  81.3 29.5 all-gather.10
  112.3 29.5 all-gather.6
  320.1 28.0 reduce-scatter.10
  401.5 26.8 reduce-scatter.8
  450.4 26.9 reduce-scatter.6
  495.6 26.8 reduce-scatter.12

commit v2 on v0

v2 whole, which is shorter than its diff:
```python
import functools

import jax
import jax.numpy as jnp
from jax import lax
from jax.experimental import pallas as pl
from jax.experimental.pallas import tpu as pltpu
from jax.sharding import PartitionSpec as P

EPSILON = 1e-05
LINK = jnp.bfloat16
F32 = jnp.float32
PAD = 128
MIB = 1 << 20


def dot_plain(left, right):
    return jnp.dot(left, right, preferred_element_type=F32)


def dot_rows(left, right):
    return lax.dot_general(left, right, (((0,), (0,)), ((), ())), preferred_element_type=F32)


def dot_last(left, right):
    return lax.dot_general(left, right, (((1,), (1,)), ((), ())), preferred_element_type=F32)


def after(v, *others):
    return lax.optimization_barrier((v, *others))[0]


def shape(dims, dtype):
    return jax.ShapeDtypeStruct(dims, dtype)


SCALARS = pl.BlockSpec(memory_space=pltpu.SMEM)
WHOLE = pl.BlockSpec(memory_space=pltpu.VMEM)


def call(kernel, scalars, args, outs, flops=0, limit=40, scratch=(), name=None):
    moved = sum(a.size * a.dtype.itemsize for a in args) + sum(
        o.size * jnp.dtype(o.dtype).itemsize for o in outs
    )
    return pl.pallas_call(
        kernel,
        out_shape=outs,
        in_specs=[SCALARS] + [WHOLE] * len(args),
        out_specs=[WHOLE] * len(outs),
        scratch_shapes=list(scratch),
        compiler_params=pltpu.CompilerParams(vmem_limit_bytes=limit * MIB),
        cost_estimate=pl.CostEstimate(flops=flops, bytes_accessed=moved, transcendentals=0),
        name=name,
    )(scalars, *args)


def pack_kernel(where_ref, in_ref, out_ref, one_ref, two_ref, taps_ref, packed_ref):
    rows = in_ref.shape[0]
    in_half, out_half = in_ref.shape[1] // 2, out_ref.shape[1] // 2
    cut = in_half + out_half
    packed_ref[:, :in_half] = in_ref[:, :in_half]
    packed_ref[:, in_half:cut] = out_ref[:, :out_half]
    packed_ref[:, cut : cut + in_half] = in_ref[:, in_half:]
    packed_ref[:, cut + in_half : 2 * cut] = out_ref[:, out_half:]
    eye = lax.broadcasted_iota(jnp.int32, (rows, rows), 0) == lax.broadcasted_iota(
        jnp.int32, (rows, rows), 1
    )
    lane = lax.broadcasted_iota(jnp.int32, (rows, PAD), 1)
    small = jnp.zeros((rows, PAD), F32)
    for k, ref in enumerate((one_ref, two_ref)):
        column = jnp.sum(jnp.where(eye, ref[...].astype(F32), 0.0), axis=1, keepdims=True)
        small = jnp.where(lane == k, column, small)
    for k in range(3):
        small = jnp.where(lane == 2 + k, taps_ref[:, k : k + 1].astype(F32), small)
    packed_ref[:, 2 * cut :] = small.astype(LINK)


def merge_kernel(where_ref, *refs):
    pieces, (first_ref, second_ref, small_ref) = refs[:-3], refs[-3:]
    rows = pieces[0].shape[0]
    high = where_ref[2]
    cut = first_ref.shape[1]
    for s, piece in enumerate(pieces):
        spot = high - s
        spot = jnp.where(spot < 0, spot + len(pieces), spot)
        at = pl.ds(pl.multiple_of(spot * rows, rows), rows)
        first_ref[at, :] = piece[:, :cut]
        second_ref[at, :] = piece[:, cut : 2 * cut]
        small_ref[at, :] = piece[:, 2 * cut :]


def natural(low, near, away, put, rows, blocks):
    def one(h, carry):
        at = pl.ds(pl.multiple_of(h * rows, rows), rows)
        put(pl.ds(pl.multiple_of((2 * h + low) * rows, rows), rows), at, near)
        put(pl.ds(pl.multiple_of((2 * h + 1 - low) * rows, rows), rows), at, away)
        return carry

    lax.fori_loop(0, blocks, one, 0)


def mixer_weights_kernel(rows, where_ref, *refs):
    pieces, (in_ref, out_ref) = refs[:16], refs[16:18]
    low, place = where_ref[0], where_ref[1]
    in_half, out_half = in_ref.shape[1] // 8, out_ref.shape[1] // 8
    for k in range(8):
        half, r = k // 4, k % 4
        block = lax.bitwise_xor(place, r)
        in_at = pl.ds(pl.multiple_of((2 * block + half) * in_half, PAD), in_half)
        out_at = pl.ds(pl.multiple_of((2 * block + half) * out_half, PAD), out_half)

        def put(to, at, ref):
            in_ref[to, in_at] = ref[at, :in_half]
            out_ref[to, out_at] = ref[at, in_half:]

        natural(low, pieces[2 * k], pieces[2 * k + 1], put, rows, pieces[0].shape[0] // rows)


def back_rows(v, steps):
    return pltpu.roll(v, steps, 0)


def ahead_rows(v, steps):
    return pltpu.roll(v, v.shape[0] - steps, 0)


def small_rows(rows, low, near_ref, away_ref, small_ref):
    def put(to, at, ref):
        small_ref[to, :] = ref[at, :].astype(F32)

    natural(low, near_ref, away_ref, put, rows, near_ref.shape[0] // rows)
    return small_ref[...].T[:8]


def mixer_kernel(
    rows,
    where_ref,
    tokens_ref,
    same_ref,
    near_ref,
    away_ref,
    *refs,
):
    pieces = refs[:16]
    normed_ref, parts_ref, scaled_ref, hidden_ref, next_ref, gains_ref = refs[16:22]
    small_ref, in_ref, outw_ref = refs[22:]
    mixer_weights_kernel(rows, where_ref, *pieces, in_ref, outw_ref)
    width = tokens_ref.shape[1]
    step = 256
    gains_ref[...] = small_rows(rows, where_ref[0], near_ref, away_ref, small_ref)
    inputs = tokens_ref[...].astype(F32)
    inverse = lax.rsqrt(jnp.mean(inputs * inputs, axis=1, keepdims=True) + EPSILON)
    normed_ref[...] = (inputs * inverse * gains_ref[0:1, :]).astype(LINK)

    def chunk(q, carry):
        at = pl.ds(pl.multiple_of(q * step, step), step)

        def part(k):
            w = in_ref[:, pl.ds(pl.multiple_of(k * width + q * step, step), step)]
            v = dot_plain(normed_ref[...], w)
            parts_ref[k, :, at] = v
            return v

        b_part = part(0)
        x_part = part(2)
        gated = b_part * x_part
        mixed = (
            gains_ref[2:3, at] * gated
            + gains_ref[3:4, at] * (back_rows(gated, 1) * same_ref[:, 0:1])
            + gains_ref[4:5, at] * (back_rows(gated, 2) * same_ref[:, 1:2])
        )
        scaled_ref[:, at] = (part(1) * mixed).astype(LINK)
        return carry

    lax.fori_loop(0, width // step, chunk, 0)

    def final(q, total):
        at = pl.ds(pl.multiple_of(q * step, step), step)
        v = tokens_ref[:, at].astype(F32) + dot_last(scaled_ref[...], outw_ref[at, :])
        hidden_ref[:, at] = v
        return total + jnp.sum(v * v, axis=1, keepdims=True)

    total = lax.fori_loop(
        0, width // step, final, jnp.zeros((tokens_ref.shape[0], 1), F32)
    )
    inverse_two = lax.rsqrt(total / width + EPSILON)
    next_ref[...] = (hidden_ref[...] * inverse_two * gains_ref[1:2, :]).astype(LINK)


def mixer_back_kernel(
    where_ref,
    own_ref,
    got_ref,
    got_far_ref,
    hidden_ref,
    cot_ref,
    same_ref,
    gains_ref,
    parts_ref,
    outw_ref,
    hidden_grad_ref,
    branch_ref,
    proj_ref,
    sums_ref,
):
    width = hidden_ref.shape[1]
    step = 256
    hidden = hidden_ref[...]
    inverse = lax.rsqrt(jnp.mean(hidden * hidden, axis=1, keepdims=True) + EPSILON)
    grad = own_ref[...].astype(F32) + got_ref[...].astype(F32) + got_far_ref[...].astype(F32)
    sums_ref[0:1, :] = jnp.zeros((1, width), F32)
    sums_ref[1:2, :] = jnp.sum(grad * (hidden * inverse), axis=0, keepdims=True)
    weighted = grad * gains_ref[1:2, :]
    mean = jnp.mean(weighted * hidden, axis=1, keepdims=True)
    total = cot_ref[...].astype(F32) + inverse * (weighted - hidden * (inverse * inverse * mean))
    hidden_grad_ref[...] = total
    branch_ref[...] = total.astype(LINK)

    def chunk(q, carry):
        at = pl.ds(pl.multiple_of(q * step, step), step)
        grad_scaled = dot_plain(branch_ref[...], outw_ref[:, at])
        b_part, c_part, x_part = (parts_ref[k, :, at] for k in range(3))
        same_one, same_two = same_ref[:, 0:1], same_ref[:, 1:2]
        gated = b_part * x_part
        back_one = back_rows(gated, 1) * same_one
        back_two = back_rows(gated, 2) * same_two
        taps = [gains_ref[2 + k : 3 + k, at] for k in range(3)]
        mixed = taps[0] * gated + taps[1] * back_one + taps[2] * back_two
        grad_mixed = grad_scaled * c_part
        sums_ref[2:3, at] = jnp.sum(grad_mixed * gated, axis=0, keepdims=True)
        sums_ref[3:4, at] = jnp.sum(grad_mixed * back_one, axis=0, keepdims=True)
        sums_ref[4:5, at] = jnp.sum(grad_mixed * back_two, axis=0, keepdims=True)
        grad_gated = (
            taps[0] * grad_mixed
            + taps[1] * ahead_rows(grad_mixed * same_one, 1)
            + taps[2] * ahead_rows(grad_mixed * same_two, 2)
        )
        for k, v in enumerate((grad_gated * x_part, grad_scaled * mixed, grad_gated * b_part)):
            proj_ref[:, pl.ds(pl.multiple_of(k * width + q * step, step), step)] = v.astype(LINK)
        return carry

    lax.fori_loop(0, width // step, chunk, 0)
    sums_ref[5:8, :] = jnp.zeros((3, width), F32)


def mixer_grads_kernel(
    rows, order, where_ref, normed_ref, proj_ref, branch_ref, scaled_ref, *refs
):
    low, place = where_ref[0], where_ref[1]
    total_ref = refs[-1]
    in_half = proj_ref.shape[1] // 8
    out_half = scaled_ref.shape[1] // 8
    for n in range(4):
        i, half = n // 2, n % 2
        block = 2 * lax.bitwise_xor(place, order[i]) + half
        in_at = pl.ds(pl.multiple_of(block * in_half, PAD), in_half)
        out_at = pl.ds(pl.multiple_of(block * out_half, PAD), out_half)
        total_ref[:, :in_half] = dot_rows(normed_ref[...], proj_ref[:, in_at])
        total_ref[:, in_half:] = dot_rows(branch_ref[...], scaled_ref[:, out_at])

        def copy(h, carry, n=n):
            to = pl.ds(pl.multiple_of(h * rows, rows), rows)
            for k, bit in enumerate((low, 1 - low)):
                at = pl.ds(pl.multiple_of((2 * h + bit) * rows, rows), rows)
                refs[2 * n + k][to, :] = total_ref[at, :].astype(LINK)
            return carry

        lax.fori_loop(0, refs[0].shape[0] // rows, copy, 0)


def add_kernel(where_ref, *refs):
    n = len(refs) // 3
    for a, b, c in zip(refs[:n], refs[n : 2 * n], refs[2 * n :]):
        c[...] = (a[...].astype(F32) + b[...].astype(F32)).astype(c.dtype)


def last_kernel(
    rows, where_ref, a_ref, a_got_ref, a_far_ref, a_row_ref, b_ref, b_got_ref, b_row_ref, b_far_ref, small_ref, *refs
):
    low, high = where_ref[0], where_ref[2]
    cut = a_ref.shape[1]
    own_ref, sends, turned_ref = refs[0], refs[1:-1], refs[-1]
    width = turned_ref.shape[0]
    turned_ref[...] = jnp.concatenate(
        [small_ref[...], jnp.zeros((PAD - 8, width), F32)], axis=0
    ).T

    def total(at, *parts):
        v = parts[0][at, :].astype(F32)
        for p in parts[1:]:
            v = v + p[at, :].astype(F32)
        return v

    for s, ref in enumerate((own_ref, *sends)):
        spot = high + s
        spot = jnp.where(spot >= len(sends) + 1, spot - len(sends) - 1, spot)
        at = pl.ds(pl.multiple_of(spot * rows, rows), rows)
        ref[:, :cut] = total(at, a_ref, a_got_ref, a_far_ref, a_row_ref).astype(ref.dtype)
        ref[:, cut : 2 * cut] = total(at, b_ref, b_got_ref, b_row_ref, b_far_ref).astype(ref.dtype)
        at = pl.ds(pl.multiple_of((2 * spot + low) * rows, rows), rows)
        ref[:, 2 * cut :] = turned_ref[at, :].astype(ref.dtype)


def mixer_input_kernel(
    rows,
    where_ref,
    tokens_ref,
    hidden_grad_ref,
    gains_ref,
    sums_ref,
    proj_ref,
    in_ref,
    input_ref,
    small_ref,
    grad_ref,
):
    width = tokens_ref.shape[1]
    step = 256
    inputs = tokens_ref[...].astype(F32)
    inverse = lax.rsqrt(jnp.mean(inputs * inputs, axis=1, keepdims=True) + EPSILON)

    def chunk(q, carry):
        at = pl.ds(pl.multiple_of(q * step, step), step)
        grad_ref[:, at] = dot_last(proj_ref[...], in_ref[at, :])
        return carry

    lax.fori_loop(0, width // step, chunk, 0)
    grad = grad_ref[...]
    row = lax.broadcasted_iota(jnp.int32, (8, width), 0)
    gain_grad = jnp.sum(grad * (inputs * inverse), axis=0, keepdims=True)
    small_ref[...] = jnp.where(row == 0, gain_grad, sums_ref[...])
    weighted = grad * gains_ref[0:1, :]
    mean = jnp.mean(weighted * inputs, axis=1, keepdims=True)
    input_ref[...] = hidden_grad_ref[...] + inverse * (
        weighted - inputs * (inverse * inverse * mean)
    )


TILE = 256


def piece_specs(pieces, count, width):
    tiles = count // TILE
    return [
        pl.BlockSpec(
            (TILE, width), lambda t, k=k: (jnp.clip(t - k * tiles, 0, tiles - 1), 0)
        )
        for k in range(pieces)
    ]


def pick(refs, tiles):
    v = refs[0][...]
    for k in range(1, len(refs)):
        v = jnp.where(pl.program_id(0) >= k * tiles, refs[k][...], v)
    return v


def put_piece(refs, tiles, v):
    for k, ref in enumerate(refs):

        @pl.when((pl.program_id(0) >= k * tiles) & (pl.program_id(0) < (k + 1) * tiles))
        def _(ref=ref):
            ref[...] = v.astype(ref.dtype)


def whole_spec(v):
    return pl.BlockSpec(v.shape, lambda t: (0, 0))


def tiled(kernel, grid, in_specs, args, out_specs, outs, flops, limit=56, scratch=()):
    moved = sum(a.size * a.dtype.itemsize for a in args) + sum(
        o.size * jnp.dtype(o.dtype).itemsize for o in outs
    )
    return pl.pallas_call(
        kernel,
        grid=(grid,),
        in_specs=in_specs,
        out_specs=out_specs,
        out_shape=outs,
        scratch_shapes=list(scratch),
        compiler_params=pltpu.CompilerParams(vmem_limit_bytes=limit * MIB),
        cost_estimate=pl.CostEstimate(flops=flops, bytes_accessed=moved, transcendentals=0),
    )(*args)


def act_kernel(tiles, rows, where_ref, *refs):
    pieces, woven, (act_ref, silu_ref, slope_ref, gate_ref, up_ref) = refs[:4], refs[4:8], refs[8:]

    @pl.when(pl.program_id(0) == 0)
    def _():
        for k, whole_ref in enumerate((gate_ref, up_ref)):

            def put(to, at, ref, whole_ref=whole_ref):
                whole_ref[to, :] = ref[at, :]

            natural(where_ref[0], *woven[2 * k : 2 * k + 2], put, rows, woven[0].shape[0] // rows)

    normed = pick(pieces, tiles)
    gate = dot_plain(normed, gate_ref[...])
    up = dot_plain(normed, up_ref[...])
    sigmoid = 1.0 / (1.0 + jnp.exp(-gate))
    silu = gate * sigmoid
    act_ref[...] = (silu * up).astype(LINK)
    silu_ref[...] = silu.astype(LINK)
    slope_ref[...] = (up * (sigmoid + silu * (1.0 - sigmoid))).astype(LINK)


def act_call(rows, scalars, pieces, woven):
    count, width = pieces[0].shape
    inner = woven[0].shape[1]
    tiles = count // TILE
    wide = pl.BlockSpec((TILE, inner), lambda t: (t, 0))
    weight = shape((width, inner), LINK)
    return tiled(
        functools.partial(act_kernel, tiles, rows),
        4 * tiles,
        [SCALARS] + piece_specs(4, count, width) + [whole_spec(v) for v in woven],
        [scalars, *pieces, *woven],
        [wide] * 3 + [whole_spec(weight)] * 2,
        [shape((4 * count, inner), LINK)] * 3 + [weight] * 2,
        16 * count * width * inner,
    )


def back_kernel(pieces, tiles, with_got, *refs):
    cots, refs = refs[:pieces], refs[pieces:]
    silu_ref, slope_ref, gate_ref, up_ref, down_ref = refs[:5]
    refs = refs[5:]
    if with_got:
        got_ref, refs = refs[0], refs[1:]
    grad_gate_ref, grad_up_ref = refs[:2]
    grad_act = dot_plain(pick(cots, tiles), down_ref[...])
    grad_up_ref[...] = (grad_act * silu_ref[...].astype(F32)).astype(LINK)
    grad_gate_ref[...] = (grad_act * slope_ref[...].astype(F32)).astype(LINK)
    back = dot_last(grad_gate_ref[...], gate_ref[...]) + dot_last(grad_up_ref[...], up_ref[...])
    if with_got:
        back = back + got_ref[...].astype(F32)
    put_piece(refs[2:], tiles, back)


def back_call(start, cots, silu, slope, gate, up, down, got=None):
    count, width = cots[0].shape
    inner = gate.shape[1]
    tiles, pieces = count // TILE, len(cots)
    wide_in = pl.BlockSpec((TILE, inner), lambda t: (t + start * tiles, 0))
    wide = pl.BlockSpec((TILE, inner), lambda t: (t, 0))
    thin = piece_specs(pieces, count, width)
    extra = [] if got is None else [got]
    return tiled(
        functools.partial(back_kernel, pieces, tiles, got is not None),
        pieces * tiles,
        thin + [wide_in] * 2 + [whole_spec(gate)] * 3 + thin[: len(extra)],
        [*cots, silu, slope, gate, up, down, *extra],
        [wide] * 2 + thin,
        [shape((pieces * count, inner), LINK)] * 2 + [shape((count, width), LINK)] * pieces,
        6 * pieces * count * width * inner,
    )


def out_kernel(tiles, act_ref, down_ref, *refs):
    put_piece(refs, tiles, dot_last(act_ref[...], down_ref[...]))


def out_call(act, down, count):
    width, inner = down.shape
    tiles = count // TILE
    return tiled(
        functools.partial(out_kernel, tiles),
        4 * tiles,
        [pl.BlockSpec((TILE, inner), lambda t: (t, 0)), whole_spec(down)],
        [act, down],
        piece_specs(4, count, width),
        [shape((count, width), LINK)] * 4,
        8 * count * width * inner,
    )


def weight_grad_kernel(rows, spots, whole, where_ref, *refs):
    lefts, refs = refs[:4], refs[4:]
    low = where_ref[0]
    count = lefts[0].shape[0]
    at = pl.ds(pl.multiple_of(pl.program_id(0) * TILE, TILE), TILE)
    total = None
    for left, (k, start) in zip(lefts, spots):
        v = dot_rows(left[:, at], refs[k][start * count : (start + 1) * count, :])
        total = v if total is None else total + v
    if whole:
        refs[-1][...] = total.astype(LINK)
        return
    near_ref, away_ref, total_ref = refs[-3:]
    total_ref[...] = total
    for h in range(near_ref.shape[0] // rows):
        to = pl.ds(h * rows, rows)
        for ref, bit in ((near_ref, low), (away_ref, 1 - low)):
            at = pl.ds(pl.multiple_of((2 * h + bit) * rows, rows), rows)
            ref[to, :] = total_ref[at, :].astype(ref.dtype)


def weight_grad(rows, scalars, lefts, rights, spots, whole=False):
    count, width = lefts[0].shape
    inner = rights[0].shape[1]
    half = pl.BlockSpec((TILE // 2, inner), lambda t: (t, 0))
    return tiled(
        functools.partial(weight_grad_kernel, rows, spots, whole),
        width // TILE,
        [SCALARS] + [whole_spec(v) for v in (*lefts, *rights)],
        [scalars, *lefts, *rights],
        [pl.BlockSpec((TILE, inner), lambda t: (t, 0))] if whole else [half, half],
        [shape((width, inner), LINK)]
        if whole
        else [shape((width // 2, inner), F32), shape((width // 2, inner), LINK)],
        8 * count * width * inner,
        scratch=[] if whole else [pltpu.VMEM((TILE, inner), F32)],
    )


def body(
    tokens,
    segments,
    mixer_gain,
    in_weight,
    conv_kernel,
    out_weight,
    ffn_gain,
    gate_weight,
    up_weight,
    down_weight,
    cotangent,
):
    count, width = tokens.shape
    rows = in_weight.shape[0]
    in_cols, out_cols = in_weight.shape[1], out_weight.shape[1]
    cut = (in_cols + out_cols) // 2
    ways = width // rows
    half = ways // 2
    columns = lax.axis_size("dp")
    place = lax.axis_index("dp")
    low = lax.rem(lax.axis_index("fsdp"), 2)
    high = lax.axis_index("fsdp") // 2
    scalars = jnp.stack([low, place, high]).astype(jnp.int32)
    strides = [[2 * h + bit for h in range(half)] for bit in range(2)]

    def swap_row(v):
        return lax.ppermute(v, "fsdp", [(i, i ^ 1) for i in range(ways)])

    def swap_far(v):
        return lax.ppermute(v, "dp", [(i, i ^ 2) for i in range(columns)])

    def swap_core(v):
        return lax.ppermute(v, "dp", [(i, i ^ 1) for i in range(columns)])

    def shift_high(v, s):
        return lax.ppermute(v, "fsdp", [(i, (i + 2 * s) % ways) for i in range(ways)])

    def gather_high(v):
        return lax.all_gather(v, "fsdp", axis=0, tiled=True, axis_index_groups=strides)

    def scatter_high(v):
        return lax.psum_scatter(
            v, "fsdp", scatter_dimension=0, tiled=True, axis_index_groups=strides
        )

    (packed,) = call(
        pack_kernel,
        scalars,
        [in_weight, out_weight, mixer_gain[None, :], ffn_gain[None, :], conv_kernel],
        [shape((rows, 2 * cut + PAD), LINK)],
    )
    shifts = [packed] + [shift_high(packed, s) for s in range(1, half)]
    tall = half * rows
    cot_far = swap_far(after(cotangent, packed))
    down_other = swap_row(after(down_weight, packed))
    down_pair = jnp.where(
        low == 0,
        jnp.concatenate([down_weight, down_other], axis=0),
        jnp.concatenate([down_other, down_weight], axis=0),
    )
    shifts[0] = after(shifts[0], cot_far, down_pair)
    first, second, small_near = call(
        merge_kernel,
        scalars,
        shifts,
        [shape((tall, cut), LINK), shape((tall, cut), LINK), shape((tall, PAD), LINK)],
    )
    gate_near = gather_high(after(gate_weight, first))
    up_near = gather_high(after(up_weight, first))
    down_all = gather_high(after(down_pair, first))
    first_row = swap_row(first)
    second_far = swap_far(second)
    small_away = swap_row(small_near)
    second_row = swap_row(second)
    first_far = swap_far(first)
    second_far_row = swap_row(second_far)
    first_row_far = swap_far(first_row)
    chip = [[[first, first_row], [first_far, first_row_far]], [[second, second_row], [second_far, second_far_row]]]
    pieces = []
    for k in range(2):
        other = [[swap_core(v) for v in pair] for pair in chip[k]]
        for pair in (chip[k][0], other[0], chip[k][1], other[1]):
            pieces += pair
    pieces[0] = after(pieces[0], gate_near, small_away)
    gate_row = swap_row(gate_near)
    up_row = swap_row(up_near)

    def gather_tokens(v, far):
        return [v, swap_core(v), far, swap_core(far)]

    cots = gather_tokens(cotangent, cot_far)

    seg_ids = segments[0]
    zero = jnp.zeros((2,), F32)
    same = jnp.stack(
        [
            jnp.concatenate([zero[:1], (seg_ids[1:] == seg_ids[:-1]).astype(F32)]),
            jnp.concatenate([zero, (seg_ids[2:] == seg_ids[:-2]).astype(F32)]),
        ],
        axis=1,
    )
    normed, parts, scaled, hidden, normed_two, gains = call(
        functools.partial(mixer_kernel, rows),
        scalars,
        [tokens, same, small_near, small_away, *pieces],
        [
            shape((count, width), LINK),
            shape((3, count, width), F32),
            shape((count, width), LINK),
            shape((count, width), F32),
            shape((count, width), LINK),
            shape((8, width), F32),
        ],
        flops=8 * count * width * width,
        scratch=[
            pltpu.VMEM((width, PAD), F32),
            pltpu.VMEM((width, columns * in_cols), LINK),
            pltpu.VMEM((width, columns * out_cols), LINK),
        ],
        limit=56,
    )
    in_all, outw_all = call(
        functools.partial(mixer_weights_kernel, rows),
        scalars,
        [after(pieces[0], normed_two), *pieces[1:]],
        [shape((width, columns * in_cols), LINK), shape((width, columns * out_cols), LINK)],
    )

    normed_two = after(normed_two, up_near, gate_row)
    normeds = gather_tokens(normed_two, swap_far(normed_two))
    act, silu, slope, gate_all, up_all = act_call(
        rows, scalars, [after(normeds[0], outw_all), *normeds[1:]], [gate_near, gate_row, up_near, up_row]
    )

    def add(*pairs):
        return call(
            add_kernel,
            scalars,
            [p[0] for p in pairs] + [p[1] for p in pairs],
            [shape(p[0].shape, LINK) for p in pairs],
        )

    def spread(near, away_got):
        total = near + away_got.astype(F32)
        return scatter_high(total.astype(LINK)).astype(F32)

    weights = (silu, slope, gate_all, up_all, down_all)
    gate_xc, up_xc, back_xc = back_call(3, [cots[3]], *weights)
    down_near, down_away = weight_grad(
        rows,
        scalars,
        [after(cots[0], back_xc), *cots[1:]],
        [act],
        [(0, 0), (0, 1), (0, 2), (0, 3)],
    )
    gate_x, up_x, back_far = back_call(
        2, [after(cots[2], down_away)], *weights, got=swap_core(back_xc)
    )
    gate_o, up_o, back_own, back_c = back_call(
        0, [after(cots[0], back_far), cots[1]], *weights
    )
    down_got = swap_row(down_away)
    back = [back_own, swap_core(back_c), swap_far(back_far)]
    spots = [(0, 0), (0, 1), (1, 0), (2, 0)]
    (up_whole,) = weight_grad(
        rows,
        scalars,
        [after(normeds[0], down_got, back[2]), *normeds[1:]],
        [up_o, up_x, up_xc],
        spots,
        whole=True,
    )
    up_pair = scatter_high(up_whole).reshape(2, rows, -1)
    up_mine = jnp.where(low == 0, up_pair[0], up_pair[1])
    up_other = jnp.where(low == 0, up_pair[1], up_pair[0])
    grad_down = spread(down_near, down_got)
    gate_near_grad, gate_away = weight_grad(
        rows,
        scalars,
        [after(normeds[0], up_whole), *normeds[1:]],
        [gate_o, gate_x, gate_xc],
        spots,
    )
    gate_got = swap_row(gate_away)

    hidden_grad, branch, proj, sums = call(
        mixer_back_kernel,
        scalars,
        [after(back[0], gate_away), *back[1:], hidden, cotangent, same, gains, parts, outw_all],
        [
            shape((count, width), F32),
            shape((count, width), LINK),
            shape((count, 3 * width), LINK),
            shape((8, width), F32),
        ],
        flops=2 * count * width * width,
        limit=48,
    )

    def mixer_grads(order, first_arg):
        return call(
            functools.partial(mixer_grads_kernel, rows, order),
            scalars,
            [first_arg, proj, branch, scaled],
            [shape((tall, cut), LINK)] * 8,
            flops=4 * count * width * width,
            scratch=[pltpu.VMEM((width, cut), F32)],
        )

    send = mixer_grads((1, 3), normed)
    got = [swap_core(v) for v in send]
    mine = mixer_grads((0, 2), after(normed, send[0], gate_got))
    a_away_far, b_away_far, a_near_far, b_away_own = add(
        *((after(mine[k], up_pair), got[k]) for k in (5, 7, 4, 3))
    )
    a_away_got = swap_far(a_away_far)
    b_away_got = swap_row(b_away_far)
    a_near_got = swap_far(a_near_far)
    b_own_got = swap_row(b_away_own)
    input_grad, sums = call(
        functools.partial(mixer_input_kernel, rows),
        scalars,
        [tokens, after(hidden_grad, a_near_far), gains, sums, proj, in_all],
        [shape((count, width), F32), shape((8, width), F32)],
        flops=6 * count * width * width,
        scratch=[pltpu.VMEM((count, width), F32)],
    )
    grad_gate = spread(after(gate_near_grad, mine[0]), gate_got)

    a_away_got = after(a_away_got, input_grad)
    sums_core = sums + swap_core(sums)
    sums_far = sums_core + swap_far(sums_core)
    a_away = (mine[1].astype(F32) + got[1].astype(F32) + a_away_got.astype(F32)).astype(LINK)
    b_far = (mine[6].astype(F32) + got[6].astype(F32) + b_away_got.astype(F32)).astype(LINK)
    a_row_got = swap_row(a_away)
    b_far_got = swap_far(b_far)
    out_own, out_c, out_x, out_xc = out_call(after(act, a_away, b_far), down_all, count)
    (out_far,) = add((after(out_x, a_row_got), swap_core(out_xc)))
    out_got, out_got_far = swap_core(out_c), swap_far(after(out_far, b_far_got, sums_far))
    up_got = swap_row(up_other)
    sums = sums_far + swap_row(sums_far)
    own, *sends = call(
        functools.partial(last_kernel, rows),
        scalars,
        [
            mine[0],
            got[0],
            a_near_got,
            a_row_got,
            mine[2],
            got[2],
            b_own_got,
            b_far_got,
            after(sums, up_got),
        ],
        [shape((rows, 2 * cut + PAD), F32)] + [shape((rows, 2 * cut + PAD), LINK)] * (half - 1),
        scratch=[pltpu.VMEM((width, PAD), F32)],
    )
    owned = own
    for s in range(1, half):
        owned = owned + shift_high(sends[s - 1], s).astype(F32)
    grad_up = up_mine.astype(F32) + up_got.astype(F32)
    result = (
        hidden + (out_own.astype(F32) + out_got.astype(F32) + out_got_far.astype(F32))
    ).astype(LINK)
    in_half = in_cols // 2
    grad_in = jnp.concatenate([owned[:, :in_half], owned[:, cut : cut + in_half]], axis=1)
    grad_outw = jnp.concatenate([owned[:, in_half:cut], owned[:, cut + in_half : 2 * cut]], axis=1)
    return (
        result,
        input_grad,
        owned[:, 2 * cut],
        grad_in,
        owned[:, 2 * cut + 2 : 2 * cut + 5],
        grad_outw,
        owned[:, 2 * cut + 1],
        grad_gate,
        grad_up,
        grad_down,
    )


def solution(mesh):
    rows_spec, cols_spec = P(("dp", "fsdp"), None), P("fsdp", "dp")
    gain_spec, taps_spec = P("fsdp"), P("fsdp", None)
    return jax.shard_map(
        body,
        mesh=mesh,
        in_specs=(
            rows_spec,
            rows_spec,
            gain_spec,
            cols_spec,
            taps_spec,
            cols_spec,
            gain_spec,
            cols_spec,
            cols_spec,
            cols_spec,
            rows_spec,
        ),
        out_specs=(
            rows_spec,
            rows_spec,
            gain_spec,
            cols_spec,
            taps_spec,
            cols_spec,
            gain_spec,
            cols_spec,
            cols_spec,
            cols_spec,
        ),
        check_vma=False,
    )
```

time: 2010 us -> 420 us (0.21)
  waiting for transfers between devices: 1730 us -> 126 us
  Pallas kernels: 0 us -> 161 us
  matrix products: 138 us -> 0 us
  blocking collectives: 90.5 us -> 0 us
  starting transfers between devices: 0.79 us -> 48.7 us
  local copies, waits for them, and re-layouts: 10.8 us -> 40.5 us
    reduce_scatter x10 -> x3, waiting for transfers between devices: 1330 us -> 0.09 us  [scatter_high(): lax.psum_scatter(v, 'fsdp', scatter_dimension=0, tiled=True, axis_index_g...]
    all_gather x9 -> x3, waiting for transfers between devices: 368 us -> 0.04 us  [gather_high(): lax.all_gather(v, 'fsdp', axis=0, tiled=True, axis_index_groups=strides)]
    pallas_call x0 -> x19, Pallas kernels: none -> 161 us  [the longest x8 98.4 us: tiled(): pl.pallas_call(kernel, grid=(grid,), in_specs=in_specs, out_specs=out_spe...]
    dot_general x15 -> x0, matrix products: 138 us -> none  [the longest x5 45.5 us: contract_rows(): lax.dot_general(left, right, (((0,), (0,)), ((), ())), preferred_element_...]
    ppermute x0 -> x56, waiting for transfers between devices: none -> 125 us  [the longest x11 72.9 us: swap_far(): return lax.ppermute(v, 'dp', [(i, i ^ 2) for i in range(columns)])]
    all_gather x4 -> x0, blocking collectives: 66.6 us -> none  [the longest x1 26 us: collect_weights(): lax.all_gather(out_weight, 'fsdp', axis=0, tiled=True)]
    ppermute x0 -> x56, starting transfers between devices: none -> 48.4 us  [the longest x25 25.8 us: swap_core(): return lax.ppermute(v, 'dp', [(i, i ^ 1) for i in range(columns)])]
    unnamed x21 -> x6, waiting for transfers between devices: 27.9 us -> 0.78 us
  transfers between devices with their start and end apart: 20 -> 62, of which waited for: 20 -> 25; matrix products, arithmetic and copies ran while one was open for 6% -> 5% of each run, Pallas kernels for 0% -> 36%
where the time goes in v2:
time: 420 us; the launch traced here: 412 us
  Pallas kernels  161 us (38%)
  waiting for transfers between devices  126 us (30%)
  starting transfers between devices  48.7 us (12%)
  local copies, waits for them, and re-layouts  40.5 us (10%)
  other arithmetic  20 us (5%)
  between operations  15.1 us (4%)
    pallas_call x8, Pallas kernels, tiled(): pl.pallas_call(kernel, grid=(grid,), in_specs=in_specs, out_specs=out_spe...  98.4 us
    ppermute x11, waiting for transfers between devices, swap_far(): return lax.ppermute(v, 'dp', [(i, i ^ 2) for i in range(columns)])  72.9 us
    pallas_call x11, Pallas kernels, call(): pl.pallas_call(kernel, out_shape=outs, in_specs=[SCALARS] + [WHOLE] * len...  62.7 us
    unnamed x146, local copies, waits for them, and re-layouts  36.6 us
    ppermute x6, waiting for transfers between devices, shift_high(): lax.ppermute(v, 'fsdp', [(i, (i + 2 * s) % ways) for i in range(ways)])  28.2 us
    ppermute x25, starting transfers between devices, swap_core(): return lax.ppermute(v, 'dp', [(i, i ^ 1) for i in range(columns)])  25.8 us
    ppermute x14, waiting for transfers between devices, swap_row(): return lax.ppermute(v, 'fsdp', [(i, i ^ 1) for i in range(ways)])  22.1 us
    ppermute x14, starting transfers between devices, swap_row(): return lax.ppermute(v, 'fsdp', [(i, i ^ 1) for i in range(ways)])  10.4 us
  transfers between devices with their start and end apart: 62, of which 25 were waited for; matrix products, arithmetic and copies ran while one was open for 5% of the time, Pallas kernels for 36%

profile of v2, /device:TPU:9, one launch (start us, length us, event | category | flops | bytes accessed | tf_op | source)
XLA Modules:
  0.0 411.7 jit_solution(6059791911191049711)
XLA Ops:
  23.0 13.2 %collective-permute-done.refs_2_.refs_0_ = bf16[512,1024]{1,0:T(8,128)(2,1)S(1)} collective-permute-done((bf16[512,1024]{1,0:T(8,128)(2,1)}, bf16[512,1024]{1,0:T(8,128)(2,1)S(1)}, u32[]{:S(2)}, u32[]{:S(2)}) %collective-permute-start) | collective-permute-done | bytes 1048608 | tf_op jit(solution)/shard_map/ppermute | solution.py:548
  47.9 12.8 %collective-permute-done.5.away_ref = bf16[512,128]{1,0:T(8,128)(2,1)S(1)} collective-permute-done((bf16[512,128]{1,0:T(8,128)(2,1)S(1)}, bf16[512,128]{1,0:T(8,128)(2,1)S(1)}, u32[]{:S(2)}, u32[]{:S(2)}) %collective-permute-start.5) | collective-permute-done | bytes 131104 | tf_op jit(solution)/shard_map/ppermute | solution.py:545
  63.2 6.7 %collective-permute-done.9.refs_4_ = bf16[512,512]{1,0:T(8,128)(2,1)S(1)} collective-permute-done((bf16[512,512]{1,0:T(8,128)(2,1)S(1)}, bf16[512,512]{1,0:T(8,128)(2,1)S(1)}, u32[]{:S(2)}, u32[]{:S(2)}) %collective-permute-start.9) | collective-permute-done | bytes 524320 | tf_op jit(solution)/shard_map/ppermute | solution.py:548
  76.0 5.2 %collective-permute-done.10.refs_5_ = bf16[512,512]{1,0:T(8,128)(2,1)} collective-permute-done((bf16[512,512]{1,0:T(8,128)(2,1)S(1)}, bf16[512,512]{1,0:T(8,128)(2,1)}, u32[]{:S(2)}, u32[]{:S(2)}) %collective-permute-start.10) | collective-permute-done | bytes 524320 | tf_op jit(solution)/shard_map/ppermute | solution.py:548
  83.2 5.2 %collective-permute-start.8 = (bf16[512,512]{1,0:T(8,128)(2,1)S(1)}, bf16[512,512]{1,0:T(8,128)(2,1)}, u32[]{:S(2)}, u32[]{:S(2)}) collective-permute-start(bf16[512,512]{1,0:T(8,128)(2,1)S(1)} %collective-permute-done.6.refs_1_), channel_id=1, source_target_pairs={{0,8},{8,0},{16,24},{24,16},{1,9},{9,1},{17,25},{25,17},{2,10},{10... | collective-permute-start | bytes 1572872 | tf_op jit(solution)/shard_map/ppermute | solution.py:551
  91.8 16.3 %shard_map.188 = (bf16[512,1024]{1,0:T(8,128)(2,1)}, f32[3,512,1024]{2,1,0:T(8,128)}, bf16[512,1024]{1,0:T(8,128)(2,1)}, f32[512,1024]{1,0:T(8,128)}, bf16[512,1024]{1,0:T(8,128)(2,1)}, /*index=5*/f32[8,1024]{1,0:T(8,128)}) custom-call(s32[3]{0:T(128)} %copy-done.44, bf16[512,1024]{1,0:T(8,128)(2,1)} %tokens_ref.3, f32[512,2]{1,0:T(8,128)} %stack.32.same_ref, ...), custom_call_target="tpu_custom_call" | custom-call | flops 4294967296 | bytes 21270528 | tf_op jit(solution)/shard_map/pallas_call | solution.py:45
  110.8 20.7 %collective-permute-done.22.refs_2_ = bf16[512,1024]{1,0:T(8,128)(2,1)S(1)} collective-permute-done((bf16[512,1024]{1,0:T(8,128)(2,1)}, bf16[512,1024]{1,0:T(8,128)(2,1)S(1)}, u32[]{:S(2)}, u32[]{:S(2)}) %collective-permute-start.22) | collective-permute-done | bytes 1048608 | tf_op jit(solution)/shard_map/ppermute | solution.py:548
  141.8 6.1 %shard_map.189 = (bf16[1024,3072]{1,0:T(8,128)(2,1)}, bf16[1024,1024]{1,0:T(8,128)(2,1)S(1)}) custom-call(s32[3]{0:T(128)S(1)} %copy-done.45, bf16[512,512]{1,0:T(8,128)(2,1)S(1)} %copy-done.16, bf16[512,512]{1,0:T(8,128)(2,1)S(1)} %copy-done.20, bf16[512,512]{1,0:T(8,128)(2,1)} %collective-permute-done.7.refs_2_, ...), custom_call_target="tpu_custom_call" | custom-call | bytes 16777216 | tf_op jit(solution)/shard_map/pallas_call | solution.py:45
  151.6 18.4 %shard_map.190 = (bf16[2048,1152]{1,0:T(8,128)(2,1)}, bf16[2048,1152]{1,0:T(8,128)(2,1)}, bf16[2048,1152]{1,0:T(8,128)(2,1)}, bf16[1024,1152]{1,0:T(8,128)(2,1)}, bf16[1024,1152]{1,0:T(8,128)(2,1)}) custom-call(s32[3]{0:T(128)} %copy-done.44, bf16[512,1024]{1,0:T(8,128)(2,1)} %get-tuple-element.135.refs_0_, bf16[512,1024]{1,0:T(8,128)(2,1)} %copy-done.69, ...), custom_call_target="tpu_custom_call" | custom-call | flops 9663676416 | bytes 27787276 | tf_op jit(solution)/shard_map/pallas_call | solution.py:375
  170.1 9.7 %shard_map.191 = (bf16[512,1152]{1,0:T(8,128)(2,1)}, bf16[512,1152]{1,0:T(8,128)(2,1)}, bf16[512,1024]{1,0:T(8,128)(2,1)}) custom-call(bf16[512,1024]{1,0:T(8,128)(2,1)} %collective-permute-done.25.refs_0_.refs_3_, bf16[2048,1152]{1,0:T(8,128)(2,1)} %get-tuple-element.119.refs_1_.refs_2_, bf16[2048,1152]{1,0:T(8,128)(2,1)} %get-tuple-element.120.refs_2_.refs_3_, ...), custom_call_target="tpu_custom_call" | custom-call | flops 3623878656 | bytes 20971520 | tf_op jit(solution)/shard_map/pallas_call | solution.py:375
  179.9 11.2 %shard_map.192 = (f32[512,1152]{1,0:T(8,128)}, bf16[512,1152]{1,0:T(8,128)(2,1)}) custom-call(s32[3]{0:T(128)} %copy-done.44, bf16[512,1024]{1,0:T(8,128)(2,1)} %cot_ref.1, bf16[512,1024]{1,0:T(8,128)(2,1)} %collective-permute-done.26.refs_1_, bf16[512,1024]{1,0:T(8,128)(2,1)} %copy-done.63, bf16[512,1024]{1,0:T(8,128)(2,1)} %collective-permute-done.25.refs_0_.refs_3_, ...), custom_call_target="tpu_custom_call" | custom-call | flops 4831838208 | bytes 12451852 | tf_op jit(solution)/shard_map/pallas_call | solution.py:375
  192.3 9.8 %shard_map.193 = (bf16[512,1152]{1,0:T(8,128)(2,1)}, bf16[512,1152]{1,0:T(8,128)(2,1)}, bf16[512,1024]{1,0:T(8,128)(2,1)}) custom-call(bf16[512,1024]{1,0:T(8,128)(2,1)} %copy-done.63, bf16[2048,1152]{1,0:T(8,128)(2,1)} %get-tuple-element.119.refs_1_.refs_2_, bf16[2048,1152]{1,0:T(8,128)(2,1)} %get-tuple-element.120.refs_2_.refs_3_, ...), custom_call_target="tpu_custom_call" | custom-call | flops 3623878656 | bytes 22020096 | tf_op jit(solution)/shard_map/pallas_call | solution.py:375
  202.4 14.6 %shard_map.194 = (bf16[1024,1152]{1,0:T(8,128)(2,1)}, bf16[1024,1152]{1,0:T(8,128)(2,1)}, bf16[512,1024]{1,0:T(8,128)(2,1)}, bf16[512,1024]{1,0:T(8,128)(2,1)}) custom-call(bf16[512,1024]{1,0:T(8,128)(2,1)} %cot_ref.1, bf16[512,1024]{1,0:T(8,128)(2,1)} %collective-permute-done.26.refs_1_, bf16[2048,1152]{1,0:T(8,128)(2,1)} %get-tuple-element.119.refs_1_.refs_2_, ...), custom_call_target="tpu_custom_call" | custom-call | flops 7247757312 | bytes 25427968 | tf_op jit(solution)/shard_map/pallas_call | solution.py:375
  218.4 7.9 %collective-permute-done.29.got_far_ref = bf16[512,1024]{1,0:T(8,128)(2,1)S(1)} collective-permute-done((bf16[512,1024]{1,0:T(8,128)(2,1)}, bf16[512,1024]{1,0:T(8,128)(2,1)S(1)}, u32[]{:S(2)}, u32[]{:S(2)}) %collective-permute-start.29) | collective-permute-done | bytes 1048608 | tf_op jit(solution)/shard_map/ppermute | solution.py:548
  226.3 11.0 %shard_map.195 = bf16[1024,1152]{1,0:T(8,128)(2,1)} custom-call(s32[3]{0:T(128)} %copy-done.44, bf16[512,1024]{1,0:T(8,128)(2,1)} %get-tuple-element.135.refs_0_, bf16[512,1024]{1,0:T(8,128)(2,1)} %copy-done.69, bf16[512,1024]{1,0:T(8,128)(2,1)} %copy-done.68, bf16[512,1024]{1,0:T(8,128)(2,1)} %copy-done.70, bf16[1024,1152]{1,0:T(8,128)(2,1)} %get-tuple-element.132.refs_4_, ...), custom_call_target="tpu_custom_call" | custom-call | flops 4831838208 | bytes 11272204 | tf_op jit(solution)/shard_map/pallas_call | solution.py:375
  242.2 11.8 %shard_map.196 = (f32[512,1152]{1,0:T(8,128)}, bf16[512,1152]{1,0:T(8,128)(2,1)}) custom-call(s32[3]{0:T(128)} %copy-done.44, bf16[512,1024]{1,0:T(8,128)(2,1)} %get-tuple-element.135.refs_0_, bf16[512,1024]{1,0:T(8,128)(2,1)} %copy-done.69, bf16[512,1024]{1,0:T(8,128)(2,1)} %copy-done.68, bf16[512,1024]{1,0:T(8,128)(2,1)} %copy-done.70, ...), custom_call_target="tpu_custom_call" | custom-call | flops 4831838208 | bytes 12451852 | tf_op jit(solution)/shard_map/pallas_call | solution.py:375
  255.2 11.8 %shard_map.197 = (f32[512,1024]{1,0:T(8,128)}, bf16[512,1024]{1,0:T(8,128)(2,1)S(1)}, bf16[512,3072]{1,0:T(8,128)(2,1)}, f32[8,1024]{1,0:T(8,128)S(1)}) custom-call(s32[3]{0:T(128)S(1)} %copy-done.46, bf16[512,1024]{1,0:T(8,128)(2,1)S(1)} %copy-done.9, bf16[512,1024]{1,0:T(8,128)(2,1)S(1)} %collective-permute-done.30.got_ref, ...), custom_call_target="tpu_custom_call" | custom-call | flops 1073741824 | bytes 21041152 | tf_op jit(solution)/shard_map/pallas_call | solution.py:45
  269.0 7.7 %shard_map.198 = (bf16[512,512]{1,0:T(8,128)(2,1)S(1)}, bf16[512,512]{1,0:T(8,128)(2,1)S(1)}, bf16[512,512]{1,0:T(8,128)(2,1)S(1)}, bf16[512,512]{1,0:T(8,128)(2...) custom-call(s32[3]{0:T(128)S(1)} %copy-done.46, ...), custom_call_target="tpu_custom_call" | custom-call | flops 2147483648 | bytes 10485760 | tf_op jit(solution)/shard_map/pallas_call | solution.py:45
  282.6 6.4 %shard_map.199 = (bf16[512,512]{1,0:T(8,128)(2,1)S(1)}, bf16[512,512]{1,0:T(8,128)(2,1)S(1)}, bf16[512,512]{1,0:T(8,128)(2,1)S(1)}, bf16[512,512]{1,0:T(8,128)(2...) custom-call(s32[3]{0:T(128)S(1)} %copy-done.46, ...), custom_call_target="tpu_custom_call" | custom-call | flops 2147483648 | bytes 10485760 | tf_op jit(solution)/shard_map/pallas_call | solution.py:45
  308.6 7.1 %shard_map.201 = (f32[512,1024]{1,0:T(8,128)}, f32[8,1024]{1,0:T(8,128)S(1)}) custom-call(s32[3]{0:T(128)S(1)} %copy-done.46, bf16[512,1024]{1,0:T(8,128)(2,1)S(1)} %copy-done.8, f32[512,1024]{1,0:T(8,128)S(1)} %copy-done.3, f32[8,1024]{1,0:T(8,128)S(1)} %copy-done.42, f32[8,1024]{1,0:T(8,128)S(1)} %get-tuple-element.167.sums_ref, ...), custom_call_target="tpu_custom_call" | custom-call | flops 3221225472 | bytes 14778368 | tf_op jit(solution)/shard_map/pallas_call | solution.py:45
  326.2 11.8 %shard_map.202 = (bf16[512,1024]{1,0:T(8,128)(2,1)}, bf16[512,1024]{1,0:T(8,128)(2,1)}, bf16[512,1024]{1,0:T(8,128)(2,1)}, bf16[512,1024]{1,0:T(8,128)(2,1)}) custom-call(bf16[2048,1152]{1,0:T(8,128)(2,1)} %get-tuple-element.174.refs_4_.act_ref, bf16[1024,1152]{1,0:T(8,128)(2,1)} %all-gather.8.cloned.1.call-done.refs_5_.refs_6_.down_ref), custom_call_target="tpu_custom_call" | custom-call | flops 4831838208 | bytes 11272192 | tf_op jit(solution)/shard_map/pallas_call | solution.py:375
  345.6 7.1 %collective-permute-done.48.a_far_ref = bf16[512,512]{1,0:T(8,128)(2,1)} collective-permute-done((bf16[512,512]{1,0:T(8,128)(2,1)}, bf16[512,512]{1,0:T(8,128)(2,1)}, u32[]{:S(2)}, u32[]{:S(2)}) %collective-permute-start.48) | collective-permute-done | bytes 524320 | tf_op jit(solution)/shard_map/ppermute | solution.py:548
  353.6 10.4 %collective-permute-done.43.b_far_ref = bf16[512,512]{1,0:T(8,128)(2,1)} collective-permute-done((bf16[512,512]{1,0:T(8,128)(2,1)}, bf16[512,512]{1,0:T(8,128)(2,1)}, u32[]{:S(2)}, u32[]{:S(2)}) %collective-permute-start.43) | collective-permute-done | bytes 524320 | tf_op jit(solution)/shard_map/ppermute | solution.py:548
  374.7 17.1 %collective-permute-done.54 = bf16[128,1152]{1,0:T(8,128)(2,1)S(1)} collective-permute-done((bf16[128,1152]{1,0:T(8,128)(2,1)S(1)}, bf16[128,1152]{1,0:T(8,128)(2,1)S(1)}, u32[]{:S(2)}, u32[]{:S(2)}) %collective-permute-start.54) | collective-permute-done | bytes 294944 | tf_op jit(solution)/shard_map/ppermute | solution.py:554
  (301 shorter events, 136.5 us)
Async XLA Ops:
  7.2 67.6 %all-gather.4.cloned.1.call-start = ((), (), s32[]{:S(2)}) async-start(), calls=%async_computation.3 | async-start | bytes 1474560 | tf_op jit(solution)/shard_map/all_gather | solution.py:557
  11.9 24.3 %collective-permute-start = (bf16[512,1024]{1,0:T(8,128)(2,1)}, bf16[512,1024]{1,0:T(8,128)(2,1)S(1)}, u32[]{:S(2)}, u32[]{:S(2)}) collective-permute-start(bf16[512,1024]{1,0:T(8,128)(2,1)} %cot_ref.1), channel_id=1, source_target_pairs={{0,16},{8,24},{16,0},{24,8},{1,17},{9,25},{17,1},{25,9},{2,18},{10... | collective-permute-start | bytes 3145736 | tf_op jit(solution)/shard_map/ppermute | solution.py:548
  16.8 26.5 %collective-permute-start.4 = (bf16[128,1152]{1,0:T(8,128)(2,1)S(1)}, bf16[128,1152]{1,0:T(8,128)(2,1)S(1)}, u32[]{:S(2)}, u32[]{:S(2)}) collective-permute-start(bf16[128,1152]{1,0:T(8,128)(2,1)S(1)} %shard_map.186.refs_0_), channel_id=1, source_target_pairs={{0,6},{1,7},{2,0},{3,1},{4,2},{5,3},{6,4},{7,5},{8,14},{9,15},{10,... | collective-permute-start | bytes 884744 | tf_op jit(solution)/shard_map/ppermute | solution.py:554
  43.9 64.2 %all-gather.6.cloned.1.call-start = ((), (), s32[]{:S(2)}) async-start(), calls=%async_computation.4 | async-start | bytes 1474560 | tf_op jit(solution)/shard_map/all_gather | solution.py:557
  44.7 125.4 %all-gather.8.cloned.1.call-start = ((), (), s32[]{:S(2)}) async-start(), calls=%async_computation.5 | async-start | bytes 2949120 | tf_op jit(solution)/shard_map/all_gather | solution.py:557
  47.7 24.2 %collective-permute-start.13 = (bf16[512,512]{1,0:T(8,128)(2,1)S(1)}, bf16[512,512]{1,0:T(8,128)(2,1)S(1)}, u32[]{:S(2)}, u32[]{:S(2)}) collective-permute-start(bf16[512,512]{1,0:T(8,128)(2,1)S(1)} %get-tuple-element.109.refs_8_), channel_id=1, source_target_pairs={{0,1},{1,0},{2,3},{3,2},{4,5},{5,4},{6,7},{7,6},{8,9},{9,8},{10,11... | collective-permute-start | bytes 1572872 | tf_op jit(solution)/shard_map/ppermute | solution.py:545
  74.8 33.3 %collective-permute-start.20 = (bf16[512,1152]{1,0:T(8,128)(2,1)}, bf16[512,1152]{1,0:T(8,128)(2,1)}, u32[]{:S(2)}, u32[]{:S(2)}) collective-permute-start(bf16[512,1152]{1,0:T(8,128)(2,1)} %all-gather.4.cloned.1.call-done.refs_4_), channel_id=1, source_target_pairs={{0,1},{1,0},{2,3},{3,2},{4,5},{5,4},{6,7},{7,6},{8,9},{9,8},{10,11... | collective-permute-start | bytes 3538952 | tf_op jit(solution)/shard_map/ppermute | solution.py:545
  89.1 207.7 %reduce-scatter.4.cloned.1.call-start = ((), (), s32[]{:S(2)}) async-start(), calls=%async_computation.6 | async-start | bytes 2949120 | tf_op jit(solution)/shard_map/reduce_scatter | solution.py:560
  108.4 40.8 %collective-permute-start.24 = (bf16[512,1152]{1,0:T(8,128)(2,1)}, bf16[512,1152]{1,0:T(8,128)(2,1)S(1)}, u32[]{:S(2)}, u32[]{:S(2)}) collective-permute-start(bf16[512,1152]{1,0:T(8,128)(2,1)} %all-gather.6.cloned.1.call-done.refs_6_), channel_id=1, source_target_pairs={{0,1},{1,0},{2,3},{3,2},{4,5},{5,4},{6,7},{7,6},{8,9},{9,8},{10,11... | collective-permute-start | bytes 3538952 | tf_op jit(solution)/shard_map/ppermute | solution.py:545
  108.7 40.6 %collective-permute-start.21 = (bf16[512,1024]{1,0:T(8,128)(2,1)}, bf16[512,1024]{1,0:T(8,128)(2,1)S(1)}, u32[]{:S(2)}, u32[]{:S(2)}) collective-permute-start(bf16[512,1024]{1,0:T(8,128)(2,1)} %get-tuple-element.135.refs_0_), channel_id=1, source_target_pairs={{0,8},{8,0},{16,24},{24,16},{1,9},{9,1},{17,25},{25,17},{2,10},{10... | collective-permute-start | bytes 3145736 | tf_op jit(solution)/shard_map/ppermute | solution.py:551
  134.0 36.1 %collective-permute-start.25 = (bf16[512,1024]{1,0:T(8,128)(2,1)}, bf16[512,1024]{1,0:T(8,128)(2,1)}, u32[]{:S(2)}, u32[]{:S(2)}) collective-permute-start(bf16[512,1024]{1,0:T(8,128)(2,1)} %copy-done.63), channel_id=1, source_target_pairs={{0,8},{8,0},{16,24},{24,16},{1,9},{9,1},{17,25},{25,17},{2,10},{10... | collective-permute-start | bytes 3145736 | tf_op jit(solution)/shard_map/ppermute | solution.py:551
  134.0 45.9 %collective-permute-start.26 = (bf16[512,1024]{1,0:T(8,128)(2,1)S(1)}, bf16[512,1024]{1,0:T(8,128)(2,1)}, u32[]{:S(2)}, u32[]{:S(2)}) collective-permute-start(bf16[512,1024]{1,0:T(8,128)(2,1)S(1)} %copy-done.6), channel_id=1, source_target_pairs={{0,8},{8,0},{16,24},{24,16},{1,9},{9,1},{17,25},{25,17},{2,10},{10... | collective-permute-start | bytes 3145736 | tf_op jit(solution)/shard_map/ppermute | solution.py:551
  191.1 27.3 %collective-permute-start.28 = (bf16[512,1152]{1,0:T(8,128)(2,1)}, bf16[512,1152]{1,0:T(8,128)(2,1)S(1)}, u32[]{:S(2)}, u32[]{:S(2)}) collective-permute-start(bf16[512,1152]{1,0:T(8,128)(2,1)} %get-tuple-element.126), channel_id=1, source_target_pairs={{0,1},{1,0},{2,3},{3,2},{4,5},{5,4},{6,7},{7,6},{8,9},{9,8},{10,11... | collective-permute-start | bytes 3538952 | tf_op jit(solution)/shard_map/ppermute | solution.py:545
  202.2 24.2 %collective-permute-start.29 = (bf16[512,1024]{1,0:T(8,128)(2,1)}, bf16[512,1024]{1,0:T(8,128)(2,1)S(1)}, u32[]{:S(2)}, u32[]{:S(2)}) collective-permute-start(bf16[512,1024]{1,0:T(8,128)(2,1)} %get-tuple-element.128), channel_id=1, source_target_pairs={{0,16},{8,24},{16,0},{24,8},{1,17},{9,25},{17,1},{25,9},{2,18},{10... | collective-permute-start | bytes 3145736 | tf_op jit(solution)/shard_map/ppermute | solution.py:548
  237.4 104.6 %reduce-scatter.8.cloned.1.call-start = ((), (), s32[]{:S(2)}) async-start(), calls=%async_computation.8 | async-start | bytes 1474560 | tf_op jit(solution)/shard_map/reduce_scatter | solution.py:560
  242.1 101.7 %reduce-scatter.6.cloned.1.call-start = ((), (), s32[]{:S(2)}) async-start(), calls=%async_computation.7 | async-start | bytes 1474560 | tf_op jit(solution)/shard_map/reduce_scatter | solution.py:560
  254.0 27.9 %collective-permute-start.31 = (bf16[512,1152]{1,0:T(8,128)(2,1)}, bf16[512,1152]{1,0:T(8,128)(2,1)S(1)}, u32[]{:S(2)}, u32[]{:S(2)}) collective-permute-start(bf16[512,1152]{1,0:T(8,128)(2,1)} %get-tuple-element.139), channel_id=1, source_target_pairs={{0,1},{1,0},{2,3},{3,2},{4,5},{5,4},{6,7},{7,6},{8,9},{9,8},{10,11... | collective-permute-start | bytes 3538952 | tf_op jit(solution)/shard_map/ppermute | solution.py:545
  281.9 39.7 %collective-permute-start.38 = (bf16[512,512]{1,0:T(8,128)(2,1)}, bf16[512,512]{1,0:T(8,128)(2,1)}, u32[]{:S(2)}, u32[]{:S(2)}) collective-permute-start(bf16[512,512]{1,0:T(8,128)(2,1)} %get-tuple-element.172), channel_id=1, source_target_pairs={{0,8},{8,0},{16,24},{24,16},{1,9},{9,1},{17,25},{25,17},{2,10},{10... | collective-permute-start | bytes 1572872 | tf_op jit(solution)/shard_map/ppermute | solution.py:551
  337.9 34.3 %collective-permute-start.42 = (bf16[512,1024]{1,0:T(8,128)(2,1)}, bf16[512,1024]{1,0:T(8,128)(2,1)S(1)}, u32[]{:S(2)}, u32[]{:S(2)}) collective-permute-start(bf16[512,1024]{1,0:T(8,128)(2,1)} %get-tuple-element.179), channel_id=1, source_target_pairs={{0,8},{8,0},{16,24},{24,16},{1,9},{9,1},{17,25},{25,17},{2,10},{10... | collective-permute-start | bytes 3145736 | tf_op jit(solution)/shard_map/ppermute | solution.py:551
  340.7 24.1 %collective-permute-start.41 = (bf16[512,512]{1,0:T(8,128)(2,1)}, bf16[512,512]{1,0:T(8,128)(2,1)}, u32[]{:S(2)}, u32[]{:S(2)}) collective-permute-start(bf16[512,512]{1,0:T(8,128)(2,1)} %add_convert_fusion.4), channel_id=1, source_target_pairs={{0,1},{1,0},{2,3},{3,2},{4,5},{5,4},{6,7},{7,6},{8,9},{9,8},{10,11... | collective-permute-start | bytes 1572872 | tf_op jit(solution)/shard_map/ppermute | solution.py:545
  367.4 24.4 %collective-permute-start.54 = (bf16[128,1152]{1,0:T(8,128)(2,1)S(1)}, bf16[128,1152]{1,0:T(8,128)(2,1)S(1)}, u32[]{:S(2)}, u32[]{:S(2)}) collective-permute-start(bf16[128,1152]{1,0:T(8,128)(2,1)S(1)} %get-tuple-element.189), channel_id=1, source_target_pairs={{0,4},{1,5},{2,6},{3,7},{4,0},{5,1},{6,2},{7,3},{8,12},{9,13},{10,... | collective-permute-start | bytes 884744 | tf_op jit(solution)/shard_map/ppermute | solution.py:554
  367.9 26.5 %collective-permute-start.55 = (bf16[128,1152]{1,0:T(8,128)(2,1)S(1)}, bf16[128,1152]{1,0:T(8,128)(2,1)S(1)}, u32[]{:S(2)}, u32[]{:S(2)}) collective-permute-start(bf16[128,1152]{1,0:T(8,128)(2,1)S(1)} %get-tuple-element.190), channel_id=1, source_target_pairs={{0,6},{1,7},{2,0},{3,1},{4,2},{5,3},{6,4},{7,5},{8,14},{9,15},{10,... | collective-permute-start | bytes 884744 | tf_op jit(solution)/shard_map/ppermute | solution.py:554
  370.2 30.9 %collective-permute-start.40 = (bf16[512,1024]{1,0:T(8,128)(2,1)}, bf16[512,1024]{1,0:T(8,128)(2,1)}, u32[]{:S(2)}, u32[]{:S(2)}) collective-permute-start(bf16[512,1024]{1,0:T(8,128)(2,1)} %get-tuple-element.176), channel_id=1, source_target_pairs={{0,8},{8,0},{16,24},{24,16},{1,9},{9,1},{17,25},{25,17},{2,10},{10... | collective-permute-start | bytes 3145736 | tf_op jit(solution)/shard_map/ppermute | solution.py:551
  373.0 28.1 %collective-permute-start.46 = (bf16[512,1024]{1,0:T(8,128)(2,1)S(1)}, bf16[512,1024]{1,0:T(8,128)(2,1)}, u32[]{:S(2)}, u32[]{:S(2)}) collective-permute-start(bf16[512,1024]{1,0:T(8,128)(2,1)S(1)} %shard_map.203), channel_id=1, source_target_pairs={{0,16},{8,24},{16,0},{24,8},{1,17},{9,25},{17,1},{25,9},{2,18},{10... | collective-permute-start | bytes 3145736 | tf_op jit(solution)/shard_map/ppermute | solution.py:548
  (110 other events, 1406.8 us)
Sparse Core Ops, SparseCore 0:
  44.0 27.8 all-gather.3
  73.5 29.5 all-gather.5
  105.2 48.4 all-gather.7
  237.5 44.9 reduce-scatter.3
  284.6 29.0 reduce-scatter.7
  315.9 27.8 reduce-scatter.5
